TPU v7x, 32 devices: a whole 2x2x4 slice. The times are simulated.
32 devices in a mesh: gx: 8 (over y, x, core), gy: 4 (over z).
Axes of the slice: x: 2, y: 2, z: 4, core: 2. Of those that a mesh axis runs over, the one named last changes fastest.
Arguments:
- volume: bfloat16 [64, 4, 128, 2048], P(None, None, 'gy', 'gx'), may hold values from -6 to 6
- brick_mask: int32 [16, 64], P('gy', 'gx'), may hold values 0 or 1
- conv1_weight: bfloat16 [64, 64, 3, 3, 3], replicated, may hold values from -0.15625 to 0.15625
- conv1_bias: float32 [64], replicated, may hold values from -3 to 3
- conv2_weight: bfloat16 [64, 64, 1, 3, 3], replicated, may hold values from -0.25 to 0.25
- conv2_bias: float32 [64], replicated, may hold values from -3 to 3
- voxel_owner: int32 [262144, 1], P(('gx', 'gy')), may hold values from 0 to 31; in each aligned block of 8192 rows (0 to 8191, 8192 to 16383, ...) at most 512 rows name the same one
- voxel_segment: int32 [262144], P(('gx', 'gy')), may hold values from 0 to 127
Outputs:
- coarse: bfloat16 [64, 4, 64, 1024], P(None, None, 'gy', 'gx')
- supervox: float32 [64, 4096], P(None, ('gx', 'gy'))
Inputs may be any that keep to these rules, and one draw needn't show every extreme that they name: `voxel_owner`: in the rows of one device no owner is named by more than 512 rows, a bound that some block reaches.
All inputs are finite; a program needn't handle non-finite values. No bound on the sum of `brick_mask` on one device may be relied on, other than what follows from the above.
Results may differ from a plain program's by a relative error of at most 0.0041.
Values may be sent and summed in bfloat16 or wider, within the bound.
A program may use at most 128 MiB of HBM per device.

v0:
```python
import math

import jax
import jax.numpy as jnp
from jax import lax
from jax.sharding import PartitionSpec as P

BY = 8
BX = 32
SEG_DEV = 128


def padded_2(x, sides, width):
    for axis, dim in sides:
        size, length = (lax.axis_size(axis), x.shape[dim])
        up = [(i, (i + 1) % size) for i in range(size - 1)]
        down = [(j, i) for i, j in up]
        last = lax.slice_in_dim(x, length - width, length, axis=dim)
        first = lax.slice_in_dim(x, 0, width, axis=dim)
        before = lax.ppermute(last, axis, up)
        after = lax.ppermute(first, axis, down)
        x = jnp.concatenate([before, x, after], axis=dim)
    return x


def from_behind(block, axis, distance):
    devices = range(lax.axis_size(axis))
    route = [(i - distance, i) for i in devices if i - distance in devices]
    return lax.ppermute(block, axis, route)


def per_device(
    volume,
    brick_mask,
    conv1_weight,
    conv1_bias,
    conv2_weight,
    conv2_bias,
    voxel_owner,
    voxel_segment,
):
    numbers = ("NCDHW", "OIDHW", "NCDHW")
    voxel_mask = jnp.repeat(jnp.repeat(brick_mask, BY, 0), BX, 1).astype(jnp.bfloat16)
    masked = volume * voxel_mask[None, None]
    padded = padded_2(masked, (("gx", 3), ("gy", 2)), 1)
    pre1 = lax.conv_general_dilated(
        padded[None],
        conv1_weight,
        (1, 1, 1),
        ((1, 1), (0, 0), (0, 0)),
        dimension_numbers=numbers,
        preferred_element_type=jnp.float32,
    )[0]
    pre1 = pre1 + conv1_bias[:, None, None, None]
    hidden = (jnp.maximum(pre1, 0.0) * voxel_mask[None, None].astype(jnp.float32)).astype(
        jnp.bfloat16
    )
    lower = from_behind(hidden[:, :, -1:, :], "gy", 1)
    widened = jnp.concatenate([lower, hidden], axis=2)
    left = from_behind(widened[:, :, :, -1:], "gx", 1)
    widened = jnp.concatenate([left, widened], axis=3)
    pre2 = lax.conv_general_dilated(
        widened[None],
        conv2_weight,
        (1, 2, 2),
        ((0, 0), (0, 0), (0, 0)),
        dimension_numbers=numbers,
        preferred_element_type=jnp.float32,
    )[0]
    coarse = jnp.maximum(pre2 + conv2_bias[:, None, None, None], 0.0).astype(jnp.bfloat16)
    channels = coarse.shape[0]
    features = coarse.reshape(channels, -1)
    voxels = features.shape[1]
    size_x = lax.axis_size("gx")
    size_y = lax.axis_size("gy")
    devices = size_x * size_y
    capacity = 2 * voxels // devices
    total_slots = devices * capacity
    block = math.gcd(voxels, 512)
    group = math.gcd(total_slots, 4096)
    blocks = voxels // block
    owner = voxel_owner[:, 0]
    labels = (voxel_segment + 1).astype(jnp.bfloat16)
    steps_idx = jnp.arange(block, dtype=jnp.int32)
    earlier = (steps_idx[:, None] > steps_idx[None, :]).astype(jnp.bfloat16)
    owner_ids = jnp.arange(devices, dtype=jnp.int32)
    group_ids = jnp.arange(group, dtype=jnp.int32)

    def place_block(carry, number):
        counts, rows_acc, ids_acc = carry
        start = number * block
        own = lax.dynamic_slice_in_dim(owner, start, block)
        hot = (own[:, None] == owner_ids[None, :]).astype(jnp.bfloat16)
        before = jnp.dot(earlier, hot, preferred_element_type=jnp.float32) + counts[None, :]
        position = jnp.sum(before * hot.astype(jnp.float32), axis=1).astype(jnp.int32)
        slot = own * capacity + position
        cols = lax.dynamic_slice_in_dim(features, start, block, 1)
        marks = lax.dynamic_slice_in_dim(labels, start, block)[None, :]
        row_parts = []
        id_parts = []
        for part_no in range(total_slots // group):
            place = (slot[:, None] == (part_no * group + group_ids)[None, :]).astype(jnp.bfloat16)
            row_parts.append(jnp.dot(cols, place, preferred_element_type=jnp.float32))
            id_parts.append(jnp.dot(marks, place, preferred_element_type=jnp.float32))
        rows_acc = rows_acc + jnp.concatenate(row_parts, axis=1)
        ids_acc = ids_acc + jnp.concatenate(id_parts, axis=1)
        counts = counts + jnp.sum(hot.astype(jnp.float32), axis=0)
        return ((counts, rows_acc, ids_acc), None)

    start_carry = (
        jnp.zeros((devices,), jnp.float32),
        jnp.zeros((channels, total_slots), jnp.float32),
        jnp.zeros((1, total_slots), jnp.float32),
    )
    (counts, rows_acc, ids_acc), unused = lax.scan(
        place_block, start_carry, jnp.arange(blocks, dtype=jnp.int32)
    )
    send_rows = rows_acc.astype(jnp.bfloat16)
    send_ids = (ids_acc - 1.0).astype(jnp.bfloat16)
    got_rows, got_ids = (
        lax.all_to_all(
            send_rows.reshape(channels, devices, capacity),
            ("gx", "gy"),
            split_axis=1,
            concat_axis=1,
            tiled=True,
        ),
        lax.all_to_all(
            send_ids.reshape(1, devices, capacity),
            ("gx", "gy"),
            split_axis=1,
            concat_axis=1,
            tiled=True,
        ),
    )
    got_rows = got_rows.reshape(channels, total_slots)
    got_ids = got_ids.reshape(total_slots).astype(jnp.int32)
    one_hot = (got_ids[:, None] == jnp.arange(SEG_DEV, dtype=jnp.int32)[None, :]).astype(
        jnp.bfloat16
    )
    sums = jnp.dot(got_rows, one_hot, preferred_element_type=jnp.float32)
    scale = lax.rsqrt(jnp.mean(sums * sums, axis=0, keepdims=True) + 1e-05)
    return (coarse, sums * scale)


def solution(mesh):
    placed = (
        P(None, None, "gy", "gx"),
        P("gy", "gx"),
        P(),
        P(),
        P(),
        P(),
        P(("gx", "gy"), None),
        P(("gx", "gy")),
    )
    return jax.shard_map(
        per_device,
        mesh=mesh,
        in_specs=placed,
        out_specs=(P(None, None, "gy", "gx"), P(None, ("gx", "gy"))),
        check_vma=False,
    )
```

profile of v0, /device:TPU:1, one launch (start us, length us, event | category | flops | bytes accessed | tf_op | source)
XLA Modules:
  0.0 665.0 jit_solution(1600267774409118270)
XLA Ops:
  1.6 15.6 %copy.94 = bf16[64,4,32,256]{0,2,3,1:T(8,128)(2,1)} copy(bf16[64,4,32,256]{3,2,1,0:T(8,128)(2,1)} %param.10) | data formatting | bytes 8388608 | tf_op args[0]
  17.3 4.7 broadcast_multiply_fusion
  22.0 4.5 collective-permute-start
  26.5 1.9 collective-permute-start.1
  28.5 3.3 collective-permute-done.1
  33.4 3.2 collective-permute-start.2
  40.2 4.0 collective-permute-done.3
  44.7 13.5 %maximum_bitcast_fusion = bf16[64,4,34,1,258]{0,2,4,1,3:T(8,128)(2,1)S(1)} fusion(bf16[64,4,1,258]{0,2,3,1:T(2,128)(2,1)S(1)} %copy.98, bf16[64,4,32,1]{0,2,3,1:T(8,128)(2,1)S(1)} %collective-permute-done.1, bf16[64,4,32,256]{0,2,3,1:T(8,128)(2,1)} %copy-done.3, bf16[64,4,32,1]{0,2,3,1:T(8,128)(2,1)S(1)} %collective-permute-done, ...), kind=kLoop, calls=%fused_computation.67 | loop fusion | flops 22456320 | bytes 8982528 | tf_op jit(solution)/shard_map/broadcast_in_dim | solution.py:47
  58.2 17.8 %copy.113 = bf16[64,4,34,1,258]{0,1,4,2,3:T(4,128)(2,1)S(1)} copy(bf16[64,4,34,1,258]{0,2,4,1,3:T(8,128)(2,1)S(1)} %maximum_bitcast_fusion) | data formatting | bytes 8982528
  76.0 6.5 pad.clone
  82.5 8.4 %copy.101 = bf16[64,4,34,1,8,33]{0,4,5,2,1,3:T(8,128)(2,1)} copy(bf16[64,4,34,1,8,33]{0,1,5,4,2,3:T(4,128)(2,1)} %bitcast.93) | data formatting | bytes 9191424 | tf_op jit(solution)/shard_map/conv_general_dilated | solution.py:46
  92.1 77.5 %broadcast_select_fusion.2 = f32[4,32,8,33,64]{4,2,3,1,0:T(8,128)} fusion(pred[8,33]{0,1:T(8,128)(4,1)S(1)} %copy-done.9, bf16[64,64,3,3,3]{1,0,4,3,2:T(8,128)(2,1)S(1)} %copy-done, bf16[64,4,34,1,7,2]{0,4,5,2,1,3:T(8,128)(2,1)S(1)} %slice.30, bf16[64,4,34,1,8,33]{0,4,5,2,1,3:T(8,128)(2,1)} %copy.101), kind=kOutput, calls=%fused_computation.81 | convolution fusion | flops 6245326848 | bytes 13711624 | tf_op jit(solution)/shard_map/conv_general_dilated | solution.py:46
  169.6 9.6 %copy.102 = f32[4,32,8,33,64]{4,1,3,2,0:T(8,128)S(1)} copy(f32[4,32,8,33,64]{4,2,3,1,0:T(8,128)} %broadcast_select_fusion.2) | data formatting | bytes 17301504 | tf_op jit(solution)/shard_map/conv_general_dilated | solution.py:46
  179.3 2.8 fusion.55
  182.6 3.2 collective-permute-start.4
  185.9 11.4 %collective-permute-done.4 = bf16[64,4,1,256]{0,2,3,1:T(2,128)(2,1)S(1)} collective-permute-done((bf16[64,4,1,256]{0,2,3,1:T(2,128)(2,1)S(1)}, bf16[64,4,1,256]{0,2,3,1:T(2,128)(2,1)S(1)}, u32[]{:S(2)}, u32[]{:S(2)}) %collective-permute-start.4) | collective-permute-done | bytes 131104 | tf_op jit(solution)/shard_map/ppermute | solution.py:29
  197.3 4.4 collective-permute-start.5
  202.8 7.2 %maximum_bitcast_fusion.1 = bf16[64,4,33,1,257]{0,2,4,1,3:T(8,128)(2,1)S(1)} fusion(bf16[64,4,32,256]{0,2,3,1:T(8,128)(2,1)} %copy-done.2, bf16[64,4,1,256]{0,2,3,1:T(2,128)(2,1)S(1)} %collective-permute-done.4, bf16[64,4,33,1]{0,2,3,1:T(8,128)(2,1)S(1)} %copy.104), kind=kLoop, calls=%fused_computation.68 | loop fusion | flops 13026816 | bytes 8684544 | tf_op jit(solution)/shard_map/broadcast_in_dim | solution.py:63
  210.0 17.2 %copy.114 = bf16[64,4,33,1,257]{0,1,4,2,3:T(4,128)(2,1)S(1)} copy(bf16[64,4,33,1,257]{0,2,4,1,3:T(8,128)(2,1)S(1)} %maximum_bitcast_fusion.1) | data formatting | bytes 8684544
  227.2 6.3 pad.2.clone
  233.6 8.4 %copy.107 = bf16[64,4,33,1,8,34]{0,4,5,2,1,3:T(8,128)(2,1)} copy(bf16[64,4,33,1,8,34]{0,1,5,4,2,3:T(4,128)(2,1)} %bitcast.94) | data formatting | bytes 9191424 | tf_op jit(solution)/shard_map/conv_general_dilated | solution.py:62
  243.2 8.3 %broadcast_select_fusion.3 = f32[4,16,8,17,64]{4,2,3,1,0:T(8,128)S(1)} fusion(pred[8,17]{0,1:T(8,128)(4,1)S(1)} %copy-done.10, bf16[64,64,1,3,3]{1,0,4,3,2:T(8,128)(2,1)S(1)} %copy-done.8, bf16[64,4,33,1,7,2]{0,4,5,2,1,3:T(8,128)(2,1)S(1)} %slice.33, bf16[64,4,33,1,8,34]{0,4,5,2,1,3:T(8,128)(2,1)} %copy.107), kind=kOutput, calls=%fused_computation.92 | convolution fusion | flops 656883712 | bytes 7134344 | tf_op jit(solution)/shard_map/conv_general_dilated | solution.py:62
  252.4 2.0 copy-done.4
  254.4 2.3 slice_bitcast_fusion.1
  256.7 4.1 copy.109
  262.4 1.8 maximum_convert_fusion
  264.3 327.2 %while.16 = (s32[]{:T(128)}, f32[32]{0:T(128)S(1)}, f32[64,16384]{1,0:T(8,128)}, f32[1,16384]{1,0:T(1,128)S(1)}, s32[16]{0:T(128)S(1)}, /*index=5*/s32[8192]{0:T...) while((s32[]{:T(128)}, f32[32]{0:T(128)S(1)}, ...), condition=%wide.region_3.4_spmd.clone.clone, body=%wide.region_0.3_spmd.clone.clone.sunk | while | flops 1130116096 | bytes 17490900 | solution.py:115
  272.4 1.8 fusion.144
  274.2 2.6 maximum_add_fusion.2
  290.8 1.8 fusion.144
  292.6 4.7 maximum_add_fusion.2
  311.4 1.8 fusion.144
  313.1 4.7 maximum_add_fusion.2
  331.9 1.8 fusion.144
  333.7 4.7 maximum_add_fusion.2
  352.5 1.8 fusion.144
  354.3 4.7 maximum_add_fusion.2
  373.0 1.8 fusion.144
  374.8 4.7 maximum_add_fusion.2
  393.6 1.8 fusion.144
  395.4 4.7 maximum_add_fusion.2
  414.1 1.8 fusion.144
  415.9 4.7 maximum_add_fusion.2
  434.7 1.8 fusion.144
  436.5 4.7 maximum_add_fusion.2
  455.3 1.8 fusion.144
  457.0 4.7 maximum_add_fusion.2
  475.8 1.8 fusion.144
  477.6 4.7 maximum_add_fusion.2
  498.1 4.7 maximum_add_fusion.2
  518.7 4.7 maximum_add_fusion.2
  539.3 4.7 maximum_add_fusion.2
  559.8 4.7 maximum_add_fusion.2
  578.6 1.8 fusion.144
  580.4 4.7 maximum_add_fusion.2
  593.5 7.1 %all-to-all-start.1 = ((bf16[32,2,256]{2,1,0:T(2,128)(2,1)}), bf16[32,2,256]{2,1,0:T(2,128)(2,1)S(1)}, u32[]{:S(2)}, u32[]{:S(2)}) async-start(bf16[32,2,256]{2,1,0:T(2,128)(2,1)} %reshape.111), calls=%async_computation.1 | async-start | bytes 65536 | tf_op jit(solution)/shard_map/all_to_all | solution.py:128
  600.6 2.4 convert_element_type.81
  604.7 2.7 all-to-all-done.1
  607.4 3.8 all-to-all-start
  611.2 2.7 fusion.76
  613.9 3.4 copy.112
  617.4 42.2 %all-to-all-done = bf16[64,32,512]{2,0,1:T(8,128)(2,1)} async-done(((bf16[64,32,512]{2,0,1:T(8,128)(2,1)}), bf16[64,32,512]{2,0,1:T(8,128)(2,1)}, u32[]{:S(2)}, u32[]{:S(2)}) %all-to-all-start) | async-done | bytes 2097184 | tf_op jit(solution)/shard_map/all_to_all | solution.py:121
  659.6 1.8 copy.116
  661.4 2.5 multiply_reduce_fusion
  (367 shorter events, 238.0 us)
Async XLA Ops:
  0.6 91.5 %copy-start = (bf16[64,64,3,3,3]{1,0,4,3,2:T(8,128)(2,1)S(1)}, bf16[64,64,3,3,3]{1,0,4,3,2:T(8,128)(2,1)}, u32[]{:S(2)}) copy-start(bf16[64,64,3,3,3]{1,0,4,3,2:T(8,128)(2,1)} %param.12) | copy-start | bytes 663556
  22.0 9.8 %copy-start.3 = (bf16[64,4,32,256]{0,2,3,1:T(8,128)(2,1)}, bf16[64,4,32,256]{0,2,3,1:T(8,128)(2,1)S(1)}, u32[]{:S(2)}) copy-start(bf16[64,4,32,256]{0,2,3,1:T(8,128)(2,1)S(1)} %broadcast_multiply_fusion) | copy-start | bytes 12582916
  22.0 6.4 collective-permute-start
  26.5 5.2 collective-permute-start.1
  33.4 6.3 collective-permute-start.2
  37.1 7.1 %collective-permute-start.3 = (bf16[64,4,1,258]{3,0,2,1:T(8,128)(2,1)S(1)}, bf16[64,4,1,258]{3,0,2,1:T(8,128)(2,1)S(1)}, u32[]{:S(2)}, u32[]{:S(2)}) collective-permute-start(bf16[64,4,1,258]{3,0,2,1:T(8,128)(2,1)S(1)} %copy.96), channel_id=1, source_target_pairs={{1,0},{2,1},{3,2},{5,4},{6,5},{7,6},{9,8},{10,9},{11,10},{13,12},{... | collective-permute-start | bytes 396296 | tf_op jit(solution)/shard_map/ppermute | solution.py:21
  82.5 9.6 %copy-start.9 = (pred[8,33]{0,1:T(8,128)(4,1)S(1)}, pred[8,33]{0,1:T(8,128)(4,1)}, u32[]{:S(2)}) copy-start(pred[8,33]{0,1:T(8,128)(4,1)} %constant.48) | copy-start | bytes 796
  169.6 9.7 %copy-start.7 = (f32[64]{0:T(128)S(1)}, f32[64]{0:T(128)}, u32[]{:S(2)}) copy-start(f32[64]{0:T(128)} %param.13) | copy-start | bytes 772
  182.1 15.2 %copy-start.2 = (bf16[64,4,32,256]{0,2,3,1:T(8,128)(2,1)}, bf16[64,4,32,256]{0,2,3,1:T(8,128)(2,1)S(1)}, u32[]{:S(2)}) copy-start(bf16[64,4,32,256]{0,2,3,1:T(8,128)(2,1)S(1)} %fusion.55) | copy-start | bytes 12582916
  182.1 19.7 %copy-start.5 = (s32[8192]{0:T(1024)S(1)}, s32[8192]{0:T(1024)}, u32[]{:S(2)}) copy-start(s32[8192]{0:T(1024)} %param.17) | copy-start | bytes 98308
  182.6 14.6 %collective-permute-start.4 = (bf16[64,4,1,256]{0,2,3,1:T(2,128)(2,1)S(1)}, bf16[64,4,1,256]{0,2,3,1:T(2,128)(2,1)S(1)}, u32[]{:S(2)}, u32[]{:S(2)}) collective-permute-start(bf16[64,4,1,256]{0,2,3,1:T(2,128)(2,1)S(1)} %slice.32), channel_id=1, source_target_pairs={{0,1},{1,2},{2,3},{4,5},{5,6},{6,7},{8,9},{9,10},{10,11},{12,13},{... | collective-permute-start | bytes 393224 | tf_op jit(solution)/shard_map/ppermute | solution.py:29
  197.3 5.5 collective-permute-start.5
  233.6 9.6 %copy-start.8 = (bf16[64,64,1,3,3]{1,0,4,3,2:T(8,128)(2,1)S(1)}, bf16[64,64,1,3,3]{1,0,4,3,2:T(8,128)(2,1)}, u32[]{:S(2)}) copy-start(bf16[64,64,1,3,3]{1,0,4,3,2:T(8,128)(2,1)} %param.14) | copy-start | bytes 221188
  233.6 9.6 %copy-start.10 = (pred[8,17]{0,1:T(8,128)(4,1)S(1)}, pred[8,17]{0,1:T(8,128)(4,1)}, u32[]{:S(2)}) copy-start(pred[8,17]{0,1:T(8,128)(4,1)} %constant.47) | copy-start | bytes 412
  252.3 2.0 copy-start.4
  254.4 8.0 %copy-start.6 = (f32[64]{0:T(128)S(1)}, f32[64]{0:T(128)}, u32[]{:S(2)}) copy-start(f32[64]{0:T(128)} %param.15) | copy-start | bytes 772
  593.5 13.9 %all-to-all-start.1 = ((bf16[32,2,256]{2,1,0:T(2,128)(2,1)}), bf16[32,2,256]{2,1,0:T(2,128)(2,1)S(1)}, u32[]{:S(2)}, u32[]{:S(2)}) async-start(bf16[32,2,256]{2,1,0:T(2,128)(2,1)} %reshape.111), calls=%async_computation.1 | async-start | bytes 65536 | tf_op jit(solution)/shard_map/all_to_all | solution.py:128
  607.4 52.3 %all-to-all-start = ((bf16[64,32,512]{2,0,1:T(8,128)(2,1)}), bf16[64,32,512]{2,0,1:T(8,128)(2,1)}, u32[]{:S(2)}, u32[]{:S(2)}) async-start(bf16[64,32,512]{2,0,1:T(8,128)(2,1)} %bitcast.77), calls=%async_computation | async-start | bytes 4194304 | tf_op jit(solution)/shard_map/all_to_all | solution.py:121
  611.2 53.4 %copy-start.1 = (bf16[64,64,3,3,3]{1,0,4,3,2:T(8,128)(2,1)S(1)}, bf16[64,64,3,3,3]{1,0,4,3,2:T(8,128)(2,1)}, u32[]{:S(2)}) copy-start(bf16[64,64,3,3,3]{1,0,4,3,2:T(8,128)(2,1)} %param.12) | copy-start | bytes 663556
where the time goes:
time: 674 us; the launch traced here: 665 us
  matrix products  291 us (43%)
  local copies, waits for them, and re-layouts  137 us (20%)
  other arithmetic  129 us (19%)
  waiting for transfers between devices  65.9 us (10%)
  starting transfers between devices  29.6 us (4%)
  loops' own time  11.6 us (2%)
    dot_general x64, matrix products, place_block(): row_parts.append(jnp.dot(cols, place, preferred_element_type=jnp.float32))  104 us
    dot_general x64, matrix products, place_block(): id_parts.append(jnp.dot(marks, place, preferred_element_type=jnp.float32))  93.6 us
    conv_general_dilated x1, matrix products, per_device(): lax.conv_general_dilated(padded[None], conv1_weight, (1, 1, 1), ((1, 1),...  77.5 us
    add x16, other arithmetic, place_block(): rows_acc = rows_acc + jnp.concatenate(row_parts, axis=1)  73.7 us
    unnamed x29, local copies, waits for them, and re-layouts  57.3 us
    all_to_all x1, waiting for transfers between devices, per_device(): lax.all_to_all(send_rows.reshape(channels, devices, capacity), ('gx', 'gy...  42.2 us
    conv_general_dilated x3, local copies, waits for them, and re-layouts, per_device(): lax.conv_general_dilated(padded[None], conv1_weight, (1, 1, 1), ((1, 1),...  19.2 us
    conv_general_dilated x5, local copies, waits for them, and re-layouts, per_device(): lax.conv_general_dilated(widened[None], conv2_weight, (1, 2, 2), ((0, 0),...  16.8 us
  transfers between devices with their start and end apart: 8, of which 7 were waited for; matrix products, arithmetic and copies ran while one was open for 2% of the time, Pallas kernels for 0%

commit v1 on v0

v1 whole, which is shorter than its diff:
```python
import jax
import jax.numpy as jnp
from jax import lax
from jax.sharding import PartitionSpec as P

BY = 8
BX = 32
SEG_DEV = 128


def halo(x, axis, dim, before, after):
    size, length = lax.axis_size(axis), x.shape[dim]
    up = [(i, i + 1) for i in range(size - 1)]
    down = [(i + 1, i) for i in range(size - 1)]
    first = lax.ppermute(lax.slice_in_dim(x, length - before, length, axis=dim), axis, up)
    parts = [first, x]
    if after:
        parts.append(lax.ppermute(lax.slice_in_dim(x, 0, after, axis=dim), axis, down))
    return jnp.concatenate(parts, axis=dim)


def per_device(volume, brick_mask, w1, b1, w2, b2, voxel_owner, voxel_segment):
    c, z, ny, nx = volume.shape
    bf16, f32 = jnp.bfloat16, jnp.float32
    mask = jnp.repeat(jnp.repeat(brick_mask, BY, 0), BX, 1).astype(bf16)
    masked = (volume * mask[None, None]).reshape(c * z, ny, nx)
    padded = halo(halo(masked, "gx", 2, 2, 1), "gy", 1, 2, 1)
    wide_mask = halo(halo(mask, "gx", 1, 1, 0), "gy", 0, 1, 0)
    offs = jnp.arange(z)[None, :] - jnp.arange(z)[:, None]
    band = jnp.stack([(offs == d - 1) for d in range(3)]).astype(bf16)
    w1b = jnp.einsum("ocdyx,dab->oacbyx", w1, band).reshape(c * z, c * z, 3, 3)
    w2b = jnp.einsum("ocyx,ab->oacbyx", w2[:, :, 0], jnp.eye(z, dtype=bf16)).reshape(
        c * z, c * z, 3, 3
    )
    numbers = ("NCHW", "OIHW", "NCHW")
    pre1 = lax.conv_general_dilated(
        padded[None], w1b, (1, 1), "VALID", dimension_numbers=numbers, preferred_element_type=f32
    )[0]
    pre1 = pre1 + jnp.repeat(b1, z)[:, None, None]
    hidden = (jnp.maximum(pre1, 0.0) * wide_mask.astype(f32)[None]).astype(bf16)
    pre2 = lax.conv_general_dilated(
        hidden[None], w2b, (2, 2), "VALID", dimension_numbers=numbers, preferred_element_type=f32
    )[0]
    coarse = jnp.maximum(pre2 + jnp.repeat(b2, z)[:, None, None], 0.0).astype(bf16)
    coarse = coarse.reshape(c, z, ny // 2, nx // 2)
    feats = coarse.reshape(c, -1)
    n = feats.shape[1]
    devices = lax.axis_size("gx") * lax.axis_size("gy")
    per = 2
    groups = devices // per
    owner = voxel_owner[:, 0]
    hi = owner // per
    col = (owner % per) * SEG_DEV + voxel_segment
    spread = jnp.where(
        hi[None, None, :] == jnp.arange(groups)[None, :, None], feats[:, None, :], jnp.zeros((), bf16)
    ).reshape(c * groups, n)
    hot = (col[:, None] == jnp.arange(per * SEG_DEV)[None, :]).astype(bf16)
    part = jnp.dot(spread, hot, preferred_element_type=f32).astype(bf16)
    part = part.reshape(c, devices, SEG_DEV)
    got = lax.all_to_all(part, ("gx", "gy"), split_axis=1, concat_axis=1, tiled=True)
    sums = jnp.sum(got.astype(f32), axis=1)
    scale = lax.rsqrt(jnp.mean(sums * sums, axis=0, keepdims=True) + 1e-05)
    return (coarse, sums * scale)


def solution(mesh):
    placed = (
        P(None, None, "gy", "gx"),
        P("gy", "gx"),
        P(),
        P(),
        P(),
        P(),
        P(("gx", "gy"), None),
        P(("gx", "gy")),
    )
    return jax.shard_map(
        per_device,
        mesh=mesh,
        in_specs=placed,
        out_specs=(P(None, None, "gy", "gx"), P(None, ("gx", "gy"))),
        check_vma=False,
    )
```

time: 674 us -> 339 us (0.50); the launches traced: 665 us -> 337 us
  matrix products: 291 us -> 21.2 us
  local copies, waits for them, and re-layouts: 137 us -> 239 us
  other arithmetic: 129 us -> 39.1 us
  waiting for transfers between devices: 65.9 us -> 14.1 us
  loops' own time: 11.6 us -> 0 us
    dot_general x145 -> x2, matrix products: 205 us -> 5.64 us  [the longest x1 4.61 us: per_device(): part = jnp.dot(spread, hot, preferred_element_type=f32).astype(bf16)]
    reshape x2 -> x5, local copies, waits for them, and re-layouts: 3.46 us -> 150 us  [the longest x1 71.2 us: per_device(): w1b = jnp.einsum('ocdyx,dab->oacbyx', w1, band).reshape(c * z, c * z, 3, 3)]
    add x112 -> x1, other arithmetic: 88.2 us -> 0.64 us  [per_device(): col = owner % per * SEG_DEV + voxel_segment]
    conv_general_dilated x2, matrix products: 85.8 us -> 15.6 us  [the longest x1 12.6 us: per_device(): lax.conv_general_dilated(padded[None], w1b, (1, 1), 'VALID', dimension_nu...]
    unnamed x29 -> x28, local copies, waits for them, and re-layouts: 57.3 us -> 0.06 us
    all_to_all x2 -> x1, waiting for transfers between devices: 44.9 us -> 14 us  [per_device(): lax.all_to_all(part, ('gx', 'gy'), split_axis=1, concat_axis=1, tiled=True)]
    transpose x0 -> x1, local copies, waits for them, and re-layouts: none -> 25.8 us  [per_device(): w1b = jnp.einsum('ocdyx,dab->oacbyx', w1, band).reshape(c * z, c * z, 3, 3)]
    dynamic_slice x64 -> x0, local copies, waits for them, and re-layouts: 22.9 us -> none  [the longest x16 12.2 us: place_block(): own = lax.dynamic_slice_in_dim(owner, start, block)]
  transfers between devices with their start and end apart: 8 -> 7, of which waited for: 7 -> 1; matrix products, arithmetic and copies ran while one was open for 2% -> 58% of each run, Pallas kernels for 0% -> 0%
where the time goes in v1:
time: 339 us; the launch traced here: 337 us
  local copies, waits for them, and re-layouts  239 us (71%)
  other arithmetic  39.1 us (12%)
  starting transfers between devices  23.4 us (7%)
  matrix products  21.2 us (6%)
  waiting for transfers between devices  14.1 us (4%)
    reshape x1, local copies, waits for them, and re-layouts, per_device(): w1b = jnp.einsum('ocdyx,dab->oacbyx', w1, band).reshape(c * z, c * z, 3, 3)  71.2 us
    reshape x1, local copies, waits for them, and re-layouts, per_device(): jnp.einsum('ocyx,ab->oacbyx', w2[:, :, 0], jnp.eye(z, dtype=bf16))  70.4 us
    transpose x1, local copies, waits for them, and re-layouts, per_device(): w1b = jnp.einsum('ocdyx,dab->oacbyx', w1, band).reshape(c * z, c * z, 3, 3)  25.8 us
    max x2, local copies, waits for them, and re-layouts, per_device(): hidden = (jnp.maximum(pre1, 0.0) * wide_mask.astype(f32)[None]).astype(bf16)  18.6 us
    conv_general_dilated x6, local copies, waits for them, and re-layouts, per_device(): lax.conv_general_dilated(hidden[None], w2b, (2, 2), 'VALID', dimension_nu...  16.8 us
    ppermute x4, starting transfers between devices, halo(): lax.ppermute(lax.slice_in_dim(x, length - before, length, axis=dim), axis...  15.3 us
    all_to_all x1, waiting for transfers between devices, per_device(): lax.all_to_all(part, ('gx', 'gy'), split_axis=1, concat_axis=1, tiled=True)  14 us
    transpose x1, other arithmetic, per_device(): jnp.einsum('ocyx,ab->oacbyx', w2[:, :, 0], jnp.eye(z, dtype=bf16))  12.6 us
  transfers between devices with their start and end apart: 7, of which 1 were waited for; matrix products, arithmetic and copies ran while one was open for 58% of the time, Pallas kernels for 0%

profile of v1, /device:TPU:1, one launch (start us, length us, event | category | flops | bytes accessed | tf_op | source)
XLA Modules:
  0.0 337.3 jit_solution(118382755761895731)
XLA Ops:
  0.6 0.7 convert_element_type.45
  1.3 0.1 broadcast_in_dim.46
  1.4 0.1 convert_element_type.47
  1.5 4.4 %broadcast_multiply_fusion = bf16[64,4,32,256]{3,2,1,0:T(8,128)(2,1)} fusion(bf16[64,4,32,256]{3,2,1,0:T(8,128)(2,1)} %param.8, bf16[32,256]{1,0:T(8,128)(2,1)S(1)} %convert_element_type.47), kind=kLoop, calls=%fused_computation.31 | loop fusion | flops 2097152 | bytes 8404992 | tf_op jit(solution)/shard_map/mul | solution.py:26
  6.0 7.6 %copy.36 = bf16[256,32,256]{0,2,1:T(8,128)(2,1)} copy(bf16[256,32,256]{2,1,0:T(8,128)(2,1)} %bitcast.61) | data formatting | bytes 8388608 | tf_op jit(solution)/shard_map/reshape | solution.py:26
  13.5 1.5 slice.29
  15.1 2.0 collective-permute-start.1
  17.0 1.6 slice.28
  18.6 4.5 %collective-permute-start = (bf16[256,32,2]{0,2,1:T(2,128)(2,1)}, bf16[256,32,2]{0,2,1:T(2,128)(2,1)}, u32[]{:S(2)}, u32[]{:S(2)}) collective-permute-start(bf16[256,32,2]{0,2,1:T(2,128)(2,1)} %slice.28), channel_id=1, source_target_pairs={{0,4},{4,8},{8,12},{12,16},{16,20},{20,24},{24,28},{1,5},{5,9},{9,... | collective-permute-start | bytes 98312 | tf_op jit(solution)/shard_map/ppermute | solution.py:15
  23.0 0.7 slice.32
  23.7 2.4 collective-permute-start.4
  26.2 0.6 fusion.31
  26.8 0.7 iota_compare_fusion.6
  27.5 12.6 %multiply_bitcast_fusion = bf16[64,4,64,4,3,3]{3,2,1,0,5,4:T(8,128)(2,1)} fusion(bf16[64,64,3,3]{1,0,3,2:T(8,128)(2,1)S(1)} %bitcast.63, bf16[4,4]{1,0:T(4,128)(2,1)S(1)} %fusion.41), kind=kLoop, calls=%fused_computation | loop fusion | flops 589824 | bytes 1253408 | tf_op jit(solution)/shard_map/ocyx,ab->oacbyx/transpose | solution.py:32
  40.1 1.0 convolution_bitcast_fusion
  41.2 70.4 %reshape.164 = bf16[256,256,3,3]{1,0,3,2:T(8,128)(2,1)S(1)} reshape(bf16[64,4,64,4,3,3]{3,2,1,0,5,4:T(8,128)(2,1)} %multiply_bitcast_fusion) | data formatting | bytes 2359296 | tf_op jit(solution)/shard_map/reshape | solution.py:32
  111.6 0.0 copy-start.11
  111.6 0.0 collective-permute-done.1
  111.6 0.0 collective-permute-done
  111.6 1.9 pad_maximum_fusion
  113.5 3.9 %collective-permute-start.2 = (bf16[256,2,259]{0,2,1:T(8,128)(2,1)}, bf16[256,2,259]{0,2,1:T(8,128)(2,1)}, u32[]{:S(2)}, u32[]{:S(2)}) collective-permute-start(bf16[256,2,259]{0,2,1:T(8,128)(2,1)} %pad_maximum_fusion), channel_id=1, source_target_pairs={{0,1},{1,2},{2,3},{4,5},{5,6},{6,7},{8,9},{9,10},{10,11},{12,13},{... | collective-permute-start | bytes 795656 | tf_op jit(solution)/shard_map/ppermute | solution.py:15
  117.4 1.4 pad_maximum_fusion.1
  118.8 1.3 collective-permute-start.3
  120.1 0.0 collective-permute-done.4
  120.1 1.3 pad_maximum_fusion.3
  121.4 4.6 %collective-permute-start.5 = (bf16[1,257]{1,0:T(2,128)(2,1)}, bf16[1,257]{1,0:T(2,128)(2,1)}, u32[]{:S(2)}, u32[]{:S(2)}) collective-permute-start(bf16[1,257]{1,0:T(2,128)(2,1)} %pad_maximum_fusion.3), channel_id=1, source_target_pairs={{0,1},{1,2},{2,3},{4,5},{5,6},{6,7},{8,9},{9,10},{10,11},{12,13},{... | collective-permute-start | bytes 1550 | tf_op jit(solution)/shard_map/ppermute | solution.py:15
  126.0 0.7 broadcast_in_dim.48
  126.7 1.4 add.57
  128.1 25.8 %copy.42 = bf16[64,4,64,4,3,3]{3,2,1,0,5,4:T(8,128)(2,1)} copy(bf16[64,4,64,4,3,3]{2,3,5,4,0,1:T(4,128)(2,1)S(1)} %convolution_bitcast_fusion) | data formatting | bytes 2359296 | tf_op jit(solution)/shard_map/ocdyx,dab->oacbyx/transpose | solution.py:31
  153.8 71.2 %reshape.163 = bf16[256,256,3,3]{1,0,3,2:T(8,128)(2,1)} reshape(bf16[64,4,64,4,3,3]{3,2,1,0,5,4:T(8,128)(2,1)} %copy.42) | data formatting | bytes 2359296 | tf_op jit(solution)/shard_map/reshape | solution.py:31
  225.0 0.1 broadcast_in_dim.50
  225.1 0.1 add.62
  225.2 0.3 add.63
  225.6 1.6 add.64
  227.1 0.8 maximum_convert_fusion.2
  227.9 3.7 %maximum_bitcast_fusion = bf16[256,35,1,259]{0,3,1,2:T(8,128)(2,1)S(1)} fusion(bf16[256,1,259]{0,2,1:T(8,128)(2,1)} %collective-permute-done.3, bf16[256,32,1]{0,2,1:T(2,128)(2,1)} %collective-permute-done.1, bf16[256,32,256]{0,2,1:T(8,128)(2,1)} %copy.36, bf16[256,32,2]{0,2,1:T(2,128)(2,1)} %collective-permute-done, ...), kind=kLoop, calls=%fused_computation.23 | loop fusion | flops 23206400 | bytes 9282560 | tf_op jit(solution)/shard_map/broadcast_in_dim | solution.py:37
  231.7 2.5 pad
  234.2 8.2 %reshape.168 = bf16[256,35,1,8,33]{0,4,3,1,2:T(8,128)(2,1)} reshape(bf16[256,35,1,264]{0,3,1,2:T(8,128)(2,1)} %pad) | data formatting | bytes 9461760 | tf_op jit(solution)/shard_map/conv_general_dilated | solution.py:36
  242.4 4.1 %copy.40 = bf16[256,35,1,8,33]{0,3,4,1,2:T(8,128)(2,1)S(1)} copy(bf16[256,35,1,8,33]{0,4,3,1,2:T(8,128)(2,1)} %reshape.168) | data formatting | bytes 9461760 | tf_op jit(solution)/shard_map/conv_general_dilated | solution.py:36
  246.5 0.1 slice.30
  246.6 12.6 %add_maximum_fusion = f32[33,8,33,256]{3,1,2,0:T(8,128)S(1)} fusion(f32[256]{0:T(256)S(1)} %copy-done.10, pred[8,33]{0,1:T(8,128)(4,1)S(1)} %copy-done.12, bf16[256,256,3,3]{1,0,3,2:T(8,128)(2,1)S(1)} %copy-done.1, bf16[256,35,1,7,2]{0,3,4,1,2:T(8,128)(2,1)S(1)} %slice.30, bf16[256,35,1,8,33]{0,3,4,1,2:T(8,128)(2,1)S(1)} %copy.40), kind=kOutput, calls=%fused_computation.8 | convolution fusion | flops 10298836992 | bytes 15083784 | tf_op jit(solution)/shard_map/conv_general_dilated | solution.py:36
  259.2 8.0 %copy.43 = f32[33,8,33,256]{3,2,1,0:T(8,128)} copy(f32[33,8,33,256]{3,1,2,0:T(8,128)S(1)} %add_maximum_fusion) | data formatting | bytes 17842176 | tf_op jit(solution)/shard_map/max | solution.py:40
  267.2 10.6 %reshape.172 = f32[33,1,264,256]{3,2,0,1:T(8,128)} reshape(f32[33,8,33,256]{3,2,1,0:T(8,128)} %copy.43) | data formatting | bytes 17842176 | tf_op jit(solution)/shard_map/max | solution.py:40
  277.8 4.8 %fusion.18 = bf16[256,33,1,257]{0,3,1,2:T(8,128)(2,1)S(1)} fusion(f32[33,1,264,256]{3,2,0,1:T(8,128)} %reshape.172, f32[33,257]{1,0:T(8,128)S(1)} %maximum_convert_fusion.2), kind=kLoop, calls=%fused_computation.24 | loop fusion | flops 4342272 | bytes 13060740 | tf_op jit(solution)/shard_map/convert_element_type | solution.py:40
  282.5 2.5 pad.2
  285.0 8.1 %reshape.175 = bf16[256,33,1,8,34]{0,4,3,1,2:T(8,128)(2,1)} reshape(bf16[256,33,1,272]{0,3,1,2:T(8,128)(2,1)} %pad.2) | data formatting | bytes 9191424 | tf_op jit(solution)/shard_map/conv_general_dilated | solution.py:41
  293.1 3.8 %copy.45 = bf16[256,33,1,8,34]{0,3,4,1,2:T(8,128)(2,1)S(1)} copy(bf16[256,33,1,8,34]{0,4,3,1,2:T(8,128)(2,1)} %reshape.175) | data formatting | bytes 9191424 | tf_op jit(solution)/shard_map/conv_general_dilated | solution.py:41
  296.9 0.1 slice.33
  297.0 3.0 fusion.24
  300.0 0.7 copy.46
  300.8 1.5 slice_bitcast_fusion
  302.3 2.5 copy.47
  304.8 1.5 squeeze.15
  306.4 2.4 maximum_convert_fusion
  308.8 1.8 broadcast_select_fusion
  310.6 0.0 copy-start.9
  310.6 4.6 %fusion.27 = bf16[1024,256]{1,0:T(8,128)(2,1)S(1)} fusion(bf16[1024,8192]{1,0:T(8,128)(2,1)S(1)} %bitcast.60, s32[8192]{0:T(1024)S(1)} %copy-done.7), kind=kOutput, calls=%fused_computation.34 | convolution fusion | flops 4297326592 | bytes 17334272 | tf_op jit(solution)/shard_map/dot_general | solution.py:58
  315.2 0.2 reshape.165
  315.4 1.0 copy.49
  316.4 4.9 %all-to-all-start = ((bf16[64,32,128]{2,0,1:T(8,128)(2,1)}), bf16[64,32,128]{2,0,1:T(8,128)(2,1)S(1)}, u32[]{:S(2)}, u32[]{:S(2)}) async-start(bf16[64,32,128]{2,0,1:T(8,128)(2,1)} %copy.49), calls=%async_computation | async-start | bytes 1048576 | tf_op jit(solution)/shard_map/all_to_all | solution.py:60
  321.3 1.2 maximum_convert_fusion.1
  322.5 14.0 %all-to-all-done = bf16[64,32,128]{2,0,1:T(8,128)(2,1)S(1)} async-done(((bf16[64,32,128]{2,0,1:T(8,128)(2,1)}), bf16[64,32,128]{2,0,1:T(8,128)(2,1)S(1)}, u32[]{:S(2)}, u32[]{:S(2)}) %all-to-all-start) | async-done | bytes 524320 | tf_op jit(solution)/shard_map/all_to_all | solution.py:60
  336.6 0.1 convert_reduce_fusion
  336.7 0.6 broadcast_multiply_fusion.1
  (35 shorter events, 0.1 us)
Async XLA Ops:
  6.0 20.2 %copy-start.5 = (s32[8192]{0:T(1024)S(1)}, s32[8192]{0:T(1024)}, u32[]{:S(2)}) copy-start(s32[8192]{0:T(1024)} %param.15) | copy-start | bytes 98308
  6.0 20.2 %copy-start.6 = (s32[8192,1]{0,1:T(1,128)S(1)}, s32[8192,1]{0,1:T(1,128)}, u32[]{:S(2)}) copy-start(s32[8192,1]{0,1:T(1,128)} %param.14) | copy-start | bytes 98308
  6.0 21.6 %copy-start.4 = (bf16[64,64,1,3,3]{1,0,4,3,2:T(8,128)(2,1)S(1)}, bf16[64,64,1,3,3]{1,0,4,3,2:T(8,128)(2,1)}, u32[]{:S(2)}) copy-start(bf16[64,64,1,3,3]{1,0,4,3,2:T(8,128)(2,1)} %param.12) | copy-start | bytes 221188
  15.1 96.6 %collective-permute-start.1 = (bf16[256,32,1]{0,2,1:T(2,128)(2,1)}, bf16[256,32,1]{0,2,1:T(2,128)(2,1)}, u32[]{:S(2)}, u32[]{:S(2)}) collective-permute-start(bf16[256,32,1]{0,2,1:T(2,128)(2,1)} %slice.29), channel_id=1, source_target_pairs={{4,0},{8,4},{12,8},{16,12},{20,16},{24,20},{28,24},{5,1},{9,5},{13... | collective-permute-start | bytes 49160 | tf_op jit(solution)/shard_map/ppermute | solution.py:18
  18.6 93.1 %collective-permute-start = (bf16[256,32,2]{0,2,1:T(2,128)(2,1)}, bf16[256,32,2]{0,2,1:T(2,128)(2,1)}, u32[]{:S(2)}, u32[]{:S(2)}) collective-permute-start(bf16[256,32,2]{0,2,1:T(2,128)(2,1)} %slice.28), channel_id=1, source_target_pairs={{0,4},{4,8},{8,12},{12,16},{16,20},{20,24},{24,28},{1,5},{5,9},{9,... | collective-permute-start | bytes 98312 | tf_op jit(solution)/shard_map/ppermute | solution.py:15
  23.7 96.4 %collective-permute-start.4 = (bf16[32,1]{1,0:T(8,128)(2,1)}, bf16[32,1]{1,0:T(8,128)(2,1)}, u32[]{:S(2)}, u32[]{:S(2)}) collective-permute-start(bf16[32,1]{1,0:T(8,128)(2,1)} %slice.32), channel_id=1, source_target_pairs={{0,4},{4,8},{8,12},{12,16},{16,20},{20,24},{24,28},{1,5},{5,9},{9,... | collective-permute-start | bytes 200 | tf_op jit(solution)/shard_map/ppermute | solution.py:15
  27.5 12.6 %copy-start.2 = (bf16[64,64,3,3,3]{1,0,4,3,2:T(8,128)(2,1)S(1)}, bf16[64,64,3,3,3]{1,0,4,3,2:T(8,128)(2,1)}, u32[]{:S(2)}) copy-start(bf16[64,64,3,3,3]{1,0,4,3,2:T(8,128)(2,1)} %param.10) | copy-start | bytes 663556
  111.6 5.8 %copy-start = (bf16[256,32,256]{0,2,1:T(8,128)(2,1)S(1)}, bf16[256,32,256]{0,2,1:T(8,128)(2,1)}, u32[]{:S(2)}) copy-start(bf16[256,32,256]{0,2,1:T(8,128)(2,1)} %copy.36) | copy-start | bytes 12582916
  111.6 14.4 %copy-start.11 = (f32[64]{0:T(128)S(1)}, f32[64]{0:T(128)}, u32[]{:S(2)}) copy-start(f32[64]{0:T(128)} %param.11) | copy-start | bytes 772
  113.5 114.4 %collective-permute-start.2 = (bf16[256,2,259]{0,2,1:T(8,128)(2,1)}, bf16[256,2,259]{0,2,1:T(8,128)(2,1)}, u32[]{:S(2)}, u32[]{:S(2)}) collective-permute-start(bf16[256,2,259]{0,2,1:T(8,128)(2,1)} %pad_maximum_fusion), channel_id=1, source_target_pairs={{0,1},{1,2},{2,3},{4,5},{5,6},{6,7},{8,9},{9,10},{10,11},{12,13},{... | collective-permute-start | bytes 795656 | tf_op jit(solution)/shard_map/ppermute | solution.py:15
  118.8 109.1 %collective-permute-start.3 = (bf16[256,1,259]{0,2,1:T(8,128)(2,1)}, bf16[256,1,259]{0,2,1:T(8,128)(2,1)}, u32[]{:S(2)}, u32[]{:S(2)}) collective-permute-start(bf16[256,1,259]{0,2,1:T(8,128)(2,1)} %pad_maximum_fusion.1), channel_id=1, source_target_pairs={{1,0},{2,1},{3,2},{5,4},{6,5},{7,6},{9,8},{10,9},{11,10},{13,12},{... | collective-permute-start | bytes 397832 | tf_op jit(solution)/shard_map/ppermute | solution.py:18
  121.4 105.7 %collective-permute-start.5 = (bf16[1,257]{1,0:T(2,128)(2,1)}, bf16[1,257]{1,0:T(2,128)(2,1)}, u32[]{:S(2)}, u32[]{:S(2)}) collective-permute-start(bf16[1,257]{1,0:T(2,128)(2,1)} %pad_maximum_fusion.3), channel_id=1, source_target_pairs={{0,1},{1,2},{2,3},{4,5},{5,6},{6,7},{8,9},{9,10},{10,11},{12,13},{... | collective-permute-start | bytes 1550 | tf_op jit(solution)/shard_map/ppermute | solution.py:15
  153.8 71.2 %copy-start.8 = (f32[64]{0:T(128)S(1)}, f32[64]{0:T(128)}, u32[]{:S(2)}) copy-start(f32[64]{0:T(128)} %param.13) | copy-start | bytes 772
  242.4 4.2 %copy-start.1 = (bf16[256,256,3,3]{1,0,3,2:T(8,128)(2,1)S(1)}, bf16[256,256,3,3]{1,0,3,2:T(8,128)(2,1)}, u32[]{:S(2)}) copy-start(bf16[256,256,3,3]{1,0,3,2:T(8,128)(2,1)} %reshape.163) | copy-start | bytes 3538948
  242.4 4.2 %copy-start.10 = (f32[256]{0:T(256)S(1)}, f32[256]{0:T(256)}, u32[]{:S(2)}) copy-start(f32[256]{0:T(256)} %add.57) | copy-start | bytes 3076
  242.4 4.2 %copy-start.12 = (pred[8,33]{0,1:T(8,128)(4,1)S(1)}, pred[8,33]{0,1:T(8,128)(4,1)}, u32[]{:S(2)}) copy-start(pred[8,33]{0,1:T(8,128)(4,1)} %constant.51) | copy-start | bytes 796
  293.1 3.9 %copy-start.13 = (pred[8,17]{0,1:T(8,128)(4,1)S(1)}, pred[8,17]{0,1:T(8,128)(4,1)}, u32[]{:S(2)}) copy-start(pred[8,17]{0,1:T(8,128)(4,1)} %constant.50) | copy-start | bytes 412
  304.8 4.0 %copy-start.3 = (pred[16,8192]{1,0:T(8,128)(4,1)S(1)}, pred[16,8192]{1,0:T(8,128)(4,1)}, u32[]{:S(2)}) copy-start(pred[16,8192]{1,0:T(8,128)(4,1)} %iota_compare_fusion.6) | copy-start | bytes 393220
  308.8 1.8 copy-start.7
  310.6 10.7 %copy-start.9 = (f32[64]{0:T(128)S(1)}, f32[64]{0:T(128)}, u32[]{:S(2)}) copy-start(f32[64]{0:T(128)} %param.13) | copy-start | bytes 772
  316.4 20.2 %all-to-all-start = ((bf16[64,32,128]{2,0,1:T(8,128)(2,1)}), bf16[64,32,128]{2,0,1:T(8,128)(2,1)S(1)}, u32[]{:S(2)}, u32[]{:S(2)}) async-start(bf16[64,32,128]{2,0,1:T(8,128)(2,1)} %copy.49), calls=%async_computation | async-start | bytes 1048576 | tf_op jit(solution)/shard_map/all_to_all | solution.py:60

commit v2 on v1

v2 whole, which is shorter than its diff:
```python
import functools

import jax
import jax.numpy as jnp
from jax import lax
from jax.experimental import pallas as pl
from jax.experimental.pallas import tpu as pltpu
from jax.sharding import PartitionSpec as P

BY = 8
BX = 32
SEG_DEV = 128
PER = 2


def shift_in(block, axis, dim, before, after):
    size, length = lax.axis_size(axis), block.shape[dim]
    up = [(i, i + 1) for i in range(size - 1)]
    down = [(i + 1, i) for i in range(size - 1)]
    first = lax.ppermute(lax.slice_in_dim(block, length - before, length, axis=dim), axis, up)
    if not after:
        return first, None
    return first, lax.ppermute(lax.slice_in_dim(block, 0, after, axis=dim), axis, down)


def block_kernel(
    vol, mask, rows_halo, sides, column, wt1, wt2, b1, b2, row_mask, col_mask, hi, col,
    coarse, part,
    parted, src, hid, w1, w2, feats, flat, spread, hot, acc,
):
    f32, bf16 = jnp.float32, jnp.bfloat16
    c, z, ny, nx = vol.shape
    half = nx // 2
    cz = c * z
    depth = 3 * cz

    def dot(a, b):
        return jnp.dot(a, b, preferred_element_type=f32)

    w1[...] = jnp.zeros_like(w1)
    w2[...] = jnp.zeros_like(w2)
    for tap in range(9):
        for zo in range(z):
            for zi in range(max(0, zo - 1), min(z, zo + 2)):
                w1[pl.ds(zo * c, c), pl.ds(tap * cz + zi * c, c)] = wt1[(zi - zo + 1) * 9 + tap]
            w2[pl.ds(zo * c, c), pl.ds(tap * cz + zo * c, c)] = wt2[tap]

    at = lax.broadcasted_iota(jnp.int32, (nx, nx), 0)
    to = lax.broadcasted_iota(jnp.int32, (nx, nx), 1)
    sort = (at == jnp.where(to < half, 2 * to, 2 * to - nx + 1)).astype(f32).astype(bf16)
    lane = lax.broadcasted_iota(jnp.int32, (1, half), 1)

    def put_row(s, first, count, even, odd):
        left = pltpu.roll(sides[0, pl.ds(first, count), :], lax.rem(half - s, half), 1)
        right = pltpu.roll(sides[1, pl.ds(first, count), :], half - 1 - s, 1)
        odd_before = jnp.where(lane == 0, left, pltpu.roll(odd, 1, 1)).astype(bf16)
        even_after = jnp.where(lane == half - 1, right, pltpu.roll(even, half - 1, 1)).astype(bf16)
        even, odd = even.astype(bf16), odd.astype(bf16)
        for tap, pair in enumerate(((odd_before, even), (even, odd), (odd, even_after))):
            where = pl.ds(pl.multiple_of(s * depth + tap * cz + first, 64), count)
            src[where, pl.ds(0, half)] = pair[0]
            src[where, pl.ds(half, half)] = pair[1]

    for number, s in enumerate((0, 1, ny + 2)):
        for first in range(0, cz, c):
            both = dot(rows_halo[number, pl.ds(first, c), :], sort)
            put_row(s, first, c, both[:, :half], both[:, half:])
    for plane in range(z):
        block = (vol[:, plane] * mask[...][None]).reshape(c * ny, nx)
        both = dot(block, sort)
        parted[0] = both[:, :half]
        parted[1] = both[:, half:]

        @pl.loop(0, ny)
        def _(y):
            take = pl.ds(y, c, stride=ny)
            put_row(y + 2, plane * c, c, parted[0, take, :], parted[1, take, :])

    edge = dot(w1[...], column[...])
    edge = jnp.maximum(edge + b1[...], 0.0) * col_mask[...]

    def hidden_row(t, places):
        got = dot(w1[...], src[pl.ds(pl.multiple_of(t * depth, depth), 3 * depth), :])
        got = jnp.maximum(got + b1[...], 0.0)
        keep = row_mask[pl.ds(t, 1), :]
        even = got[:, :half] * keep
        odd = got[:, half:] * keep
        first = pltpu.roll(edge, lax.rem(half - t, half), 1)
        before = jnp.where(lane == 0, first, pltpu.roll(odd, 1, 1)).astype(bf16)
        parts = (before, even.astype(bf16), odd.astype(bf16))
        for p, dy, side in places:
            for tap in range(3):
                where = pl.multiple_of((p * 9 + dy * 3 + tap) * cz, cz)
                hid[pl.ds(where, cz), pl.ds(side * half, half)] = parts[tap]

    hidden_row(0, ((0, 0, 0),))

    @pl.loop(0, ny // 4)
    def _(p):
        t = 4 * p + 1
        hidden_row(t, ((p, 1, 0),))
        hidden_row(t + 1, ((p, 2, 0), (p, 0, 1)))
        hidden_row(t + 2, ((p, 1, 1),))
        hidden_row(t + 3, ((p, 2, 1), (p + 1, 0, 0)))
        got = dot(w2[...], hid[pl.ds(pl.multiple_of(p * 9 * cz, cz), 9 * cz), :])
        got = jnp.maximum(got + b2[...], 0.0).astype(bf16)
        feats[:, pl.ds(pl.multiple_of(p * nx, nx), nx)] = got
        wide = got.astype(f32)
        flat[pl.ds(2 * p, cz, stride=ny // 2), :] = wide[:, :half]
        flat[pl.ds(2 * p + 1, cz, stride=ny // 2), :] = wide[:, half:]

    for plane in range(z):
        piece = flat[pl.ds(plane * c * ny // 2, c * ny // 2), :]
        coarse[:, plane] = piece.reshape(c, ny // 2, half).astype(bf16)

    voxels = feats.shape[1]
    groups = part.shape[0] // PER
    chunk = spread.shape[0] // c

    @pl.loop(0, groups // chunk)
    def _(g):
        for plane in range(z):
            which = col[pl.ds(plane, 1), :]
            ids = lax.broadcasted_iota(jnp.int32, (PER * SEG_DEV, 1), 0)
            hot[...] = (ids == which).astype(f32).astype(bf16)
            owner = hi[pl.ds(plane, 1), :]
            for a in range(chunk):
                on = (owner == g * chunk + a).astype(f32).astype(bf16)
                spread[pl.ds(a * c, c), :] = feats[pl.ds(plane * c, c), :] * on
            got = lax.dot_general(
                spread[...], hot[...], (((1,), (1,)), ((), ())), preferred_element_type=f32
            )
            if plane == 0:
                acc[...] = got
            else:
                acc[...] += got
        for a in range(chunk):
            for n in range(PER):
                part[(g * chunk + a) * PER + n] = acc[
                    pl.ds(a * c, c), pl.ds(n * SEG_DEV, SEG_DEV)
                ].astype(bf16)


def per_device(volume, brick_mask, w1, b1, w2, b2, voxel_owner, voxel_segment):
    c, z, ny, nx = volume.shape
    bf16, f32 = jnp.bfloat16, jnp.float32
    half, cz = nx // 2, c * z
    devices = lax.axis_size("gx") * lax.axis_size("gy")
    mask = jnp.repeat(jnp.repeat(brick_mask, BY, 0), BX, 1).astype(bf16)

    def planes(y0, y1, x0, x1):
        return volume[:, :, y0:y1, x0:x1] * mask[None, None, y0:y1, x0:x1]

    up = [(i, i + 1) for i in range(lax.axis_size("gy") - 1)]
    down = [(i + 1, i) for i in range(lax.axis_size("gy") - 1)]
    above = lax.ppermute(planes(ny - 2, ny, 0, nx).transpose(2, 1, 0, 3), "gy", up)
    below = lax.ppermute(planes(0, 1, 0, nx).transpose(2, 1, 0, 3), "gy", down)
    rows_halo = jnp.concatenate([above, below]).reshape(3, cz, nx)

    def columns(x0, x1):
        mine = planes(0, ny, x0, x1).transpose(3, 1, 0, 2).reshape(x1 - x0, cz, ny)
        top = rows_halo[:2, :, x0:x1].transpose(2, 1, 0)
        return jnp.concatenate([mine, top, rows_halo[2:, :, x0:x1].transpose(2, 1, 0)], 2)

    left, right, own = columns(nx - 2, nx), columns(0, 1), columns(0, 1)
    right_way = [(i, i + 1) for i in range(lax.axis_size("gx") - 1)]
    left_way = [(i + 1, i) for i in range(lax.axis_size("gx") - 1)]
    left = lax.ppermute(left, "gx", right_way)
    right = lax.ppermute(right, "gx", left_way)
    lines = jnp.concatenate([left, own, right])
    lines = jnp.concatenate([lines[:, :, ny : ny + 2], lines[:, :, :ny], lines[:, :, ny + 2 :]], 2)
    lines = jnp.pad(lines, ((0, 0), (0, 0), (0, half - lines.shape[2] + 2)))
    column = jnp.concatenate([lines[:3, :, d : d + half].reshape(3 * cz, half) for d in range(3)])
    sides = jnp.stack([lines[1, :, :half], lines[3, :, :half]]).astype(f32)

    marks_y = lax.ppermute(brick_mask[-1:], "gy", up)
    bricks = jnp.concatenate([marks_y, brick_mask])
    marks_x = lax.ppermute(bricks[:, -1:], "gx", right_way)
    tall = jnp.concatenate([bricks[:1], jnp.repeat(bricks[1:], BY, 0)])
    row_mask = jnp.repeat(tall, BX // 2, 1).astype(f32)
    row_mask = jnp.pad(row_mask, ((0, 7), (0, 0)))
    col_mask = jnp.concatenate([marks_x[:1], jnp.repeat(marks_x[1:], BY, 0)]).astype(f32)
    col_mask = jnp.pad(col_mask.T, ((0, 0), (0, half - ny - 1)))

    wt1 = w1.transpose(2, 3, 4, 0, 1).reshape(27, c, c)
    wt2 = w2[:, :, 0].transpose(2, 3, 0, 1).reshape(9, c, c)
    tall1 = jnp.tile(b1, z)[:, None]
    tall2 = jnp.tile(b2, z)[:, None]
    owner = voxel_owner.reshape(z, -1)
    hi = owner // PER
    col = (owner % PER) * SEG_DEV + voxel_segment.reshape(z, -1)
    voxels = owner.shape[1]
    groups = devices // PER
    chunk = min(groups, 16)

    coarse, part = pl.pallas_call(
        block_kernel,
        out_shape=(
            jax.ShapeDtypeStruct((c, z, ny // 2, half), bf16),
            jax.ShapeDtypeStruct((devices, c, SEG_DEV), bf16),
        ),
        in_specs=[pl.BlockSpec(memory_space=pltpu.VMEM)] * 13,
        out_specs=[pl.BlockSpec(memory_space=pltpu.VMEM)] * 2,
        scratch_shapes=[
            pltpu.VMEM((2, c * ny, half), f32),
            pltpu.VMEM(((ny + 3) * 3 * cz, nx), bf16),
            pltpu.VMEM(((ny // 4 * 9 + 3) * cz, nx), bf16),
            pltpu.VMEM((cz, 9 * cz), bf16),
            pltpu.VMEM((cz, 9 * cz), bf16),
            pltpu.VMEM((cz, voxels), bf16),
            pltpu.VMEM((cz * ny // 2, half), f32),
            pltpu.VMEM((chunk * c, voxels), bf16),
            pltpu.VMEM((PER * SEG_DEV, voxels), bf16),
            pltpu.VMEM((chunk * c, PER * SEG_DEV), f32),
        ],
        compiler_params=pltpu.CompilerParams(vmem_limit_bytes=56 * 1024 * 1024),
    )(
        volume, mask, rows_halo, sides, column, wt1, wt2, tall1, tall2, row_mask, col_mask, hi, col
    )
    got = lax.all_to_all(part, ("gx", "gy"), split_axis=0, concat_axis=0, tiled=True)
    sums = jnp.sum(got.astype(f32), axis=0)
    scale = lax.rsqrt(jnp.mean(sums * sums, axis=0, keepdims=True) + 1e-05)
    return (coarse, sums * scale)


def solution(mesh):
    placed = (
        P(None, None, "gy", "gx"),
        P("gy", "gx"),
        P(),
        P(),
        P(),
        P(),
        P(("gx", "gy"), None),
        P(("gx", "gy")),
    )
    return jax.shard_map(
        per_device,
        mesh=mesh,
        in_specs=placed,
        out_specs=(P(None, None, "gy", "gx"), P(None, ("gx", "gy"))),
        check_vma=False,
    )
```

time: 339 us -> 126 us (0.37)
  local copies, waits for them, and re-layouts: 239 us -> 15.4 us
  Pallas kernels: 0 us -> 52.7 us
  other arithmetic: 39.1 us -> 13.2 us
  matrix products: 21.2 us -> 0 us
  blocking collectives: 0 us -> 20.8 us
  waiting for transfers between devices: 14.1 us -> 1.72 us
    reshape x5, local copies, waits for them, and re-layouts: 150 us -> 1.09 us  [the longest x1 0.78 us: per_device(): col = owner % PER * SEG_DEV + voxel_segment.reshape(z, -1)]
    pallas_call x0 -> x1, Pallas kernels: none -> 52.7 us  [per_device(): pl.pallas_call(block_kernel, out_shape=(jax.ShapeDtypeStruct((c, z, ny //...]
    conv_general_dilated x9 -> x0, local copies, waits for them, and re-layouts: 29.1 us -> none  [the longest x6 16.8 us: per_device(): lax.conv_general_dilated(hidden[None], w2b, (2, 2), 'VALID', dimension_nu...]
    all_to_all x0 -> x1, blocking collectives: none -> 20.8 us  [per_device(): lax.all_to_all(part, ('gx', 'gy'), split_axis=0, concat_axis=0, tiled=True)]
    transpose x1 -> x8, local copies, waits for them, and re-layouts: 25.8 us -> 5.35 us  [the longest x2 4.81 us: columns(): mine = planes(0, ny, x0, x1).transpose(3, 1, 0, 2).reshape(x1 - x0, cz, ny)]
    max x2 -> x0, local copies, waits for them, and re-layouts: 18.6 us -> none  [per_device(): hidden = (jnp.maximum(pre1, 0.0) * wide_mask.astype(f32)[None]).astype(bf16)]
    conv_general_dilated x2 -> x0, matrix products: 15.6 us -> none  [the longest x1 12.6 us: per_device(): lax.conv_general_dilated(padded[None], w1b, (1, 1), 'VALID', dimension_nu...]
    all_to_all x1 -> x0, waiting for transfers between devices: 14 us -> none  [per_device(): lax.all_to_all(part, ('gx', 'gy'), split_axis=1, concat_axis=1, tiled=True)]
  transfers between devices with their start and end apart: 7 -> 6, of which waited for: 1 -> 1; matrix products, arithmetic and copies ran while one was open for 58% -> 19% of each run, Pallas kernels for 0% -> 0%
where the time goes in v2:
time: 126 us; the launch traced here: 125 us
  Pallas kernels  52.7 us (42%)
  blocking collectives  20.8 us (17%)
  starting transfers between devices  20.1 us (16%)
  local copies, waits for them, and re-layouts  15.4 us (12%)
  other arithmetic  13.2 us (10%)
  waiting for transfers between devices  1.72 us (1%)
    pallas_call x1, Pallas kernels, per_device(): pl.pallas_call(block_kernel, out_shape=(jax.ShapeDtypeStruct((c, z, ny //...  52.7 us
    all_to_all x1, blocking collectives, per_device(): lax.all_to_all(part, ('gx', 'gy'), split_axis=0, concat_axis=0, tiled=True)  20.8 us
    transpose x2, local copies, waits for them, and re-layouts, columns(): mine = planes(0, ny, x0, x1).transpose(3, 1, 0, 2).reshape(x1 - x0, cz, ny)  4.81 us
    ppermute x1, starting transfers between devices, per_device(): marks_x = lax.ppermute(bricks[:, -1:], 'gx', right_way)  4.51 us
    ppermute x1, starting transfers between devices, per_device(): left = lax.ppermute(left, 'gx', right_way)  4.19 us
    transpose x2, other arithmetic, columns(): mine = planes(0, ny, x0, x1).transpose(3, 1, 0, 2).reshape(x1 - x0, cz, ny)  4.06 us
    ppermute x1, starting transfers between devices, per_device(): marks_y = lax.ppermute(brick_mask[-1:], 'gy', up)  4.02 us
    ppermute x1, starting transfers between devices, per_device(): lax.ppermute(planes(ny - 2, ny, 0, nx).transpose(2, 1, 0, 3), 'gy', up)  4 us
  transfers between devices with their start and end apart: 6, of which 1 were waited for; matrix products, arithmetic and copies ran while one was open for 19% of the time, Pallas kernels for 0%

profile of v2, /device:TPU:1, one launch (start us, length us, event | category | flops | bytes accessed | tf_op | source)
XLA Modules:
  0.0 124.8 jit_solution(2156020662871714862)
XLA Ops:
  0.6 0.7 slice.108
  1.3 4.0 %collective-permute-start.4 = (s32[1,8]{1,0:T(1,128)S(1)}, s32[1,8]{1,0:T(1,128)S(1)}, u32[]{:S(2)}, u32[]{:S(2)}) collective-permute-start(s32[1,8]{1,0:T(1,128)S(1)} %slice.108), channel_id=1, source_target_pairs={{0,1},{1,2},{2,3},{4,5},{5,6},{6,7},{8,9},{9,10},{10,11},{12,13},{... | collective-permute-start | bytes 104 | tf_op jit(solution)/shard_map/ppermute | solution.py:176
  5.3 0.8 copy.75
  6.1 0.1 broadcast_in_dim.23
  6.2 0.1 reshape.103
  6.3 0.1 slice_reduce_fusion.2
  6.4 0.1 broadcast_in_dim.26
  6.5 0.1 mul.59
  6.5 1.4 %multiply_bitcast_fusion.2 = bf16[1,4,64,256]{3,0,1,2:T(2,128)(2,1)S(1)} fusion(bf16[64,4,32,256]{3,2,1,0:T(8,128)(2,1)} %vol.1, bf16[256]{0:T(256)(128)(2,1)S(1)} %mul.59), kind=kLoop, calls=%fused_computation.10 | loop fusion | flops 65536 | bytes 262656 | tf_op jit(solution)/shard_map/transpose | solution.py:157
  8.0 1.3 %collective-permute-start.1 = (bf16[1,4,64,256]{3,0,1,2:T(2,128)(2,1)S(1)}, bf16[1,4,64,256]{3,0,1,2:T(2,128)(2,1)S(1)}, u32[]{:S(2)}, u32[]{:S(2)}) collective-permute-start(bf16[1,4,64,256]{3,0,1,2:T(2,128)(2,1)S(1)} %multiply_bitcast_fusion.2), channel_id=1, source_target_pairs={{1,0},{2,1},{3,2},{5,4},{6,5},{7,6},{9,8},{10,9},{11,10},{13,12},{... | collective-permute-start | bytes 393224 | tf_op jit(solution)/shard_map/ppermute | solution.py:157
  9.3 0.1 slice.87
  9.3 0.1 copy.77
  9.4 0.1 broadcast_in_dim.25
  9.5 0.1 slice.88
  9.6 1.6 %multiply_bitcast_fusion.3 = bf16[2,4,64,256]{3,0,1,2:T(2,128)(2,1)S(1)} fusion(bf16[64,4,32,256]{3,2,1,0:T(8,128)(2,1)} %vol.1, bf16[2,256]{1,0:T(2,128)(2,1)S(1)} %slice.88), kind=kLoop, calls=%fused_computation.11 | loop fusion | flops 131072 | bytes 525312 | tf_op jit(solution)/shard_map/transpose | solution.py:156
  11.2 4.0 %collective-permute-start = (bf16[2,4,64,256]{3,0,1,2:T(2,128)(2,1)S(1)}, bf16[2,4,64,256]{3,0,1,2:T(2,128)(2,1)S(1)}, u32[]{:S(2)}, u32[]{:S(2)}) collective-permute-start(bf16[2,4,64,256]{3,0,1,2:T(2,128)(2,1)S(1)} %multiply_bitcast_fusion.3), channel_id=1, source_target_pairs={{0,1},{1,2},{2,3},{4,5},{5,6},{6,7},{8,9},{9,10},{10,11},{12,13},{... | collective-permute-start | bytes 786440 | tf_op jit(solution)/shard_map/ppermute | solution.py:156
  15.3 0.1 copy.76
  15.3 0.1 broadcast_in_dim.24
  15.5 0.1 convert_element_type.37.mask
  15.6 0.1 slice_reduce_fusion
  15.7 0.1 slice.113
  15.8 0.5 broadcast.76
  16.3 1.5 %reduce.9 = s32[8192]{0:T(1024)S(1)} reduce(s32[8192,1]{0,1:T(1,128)} %param.14, s32[]{:T(128)} %broadcast.76), dimensions={1}, to_apply=%param.14.reduce_sub_computation.3 | reduce | bytes 65540 | tf_op args[6]
  17.8 0.8 reshape.113
  18.6 0.7 tile.5
  19.2 0.8 broadcast_in_dim_tile.9.b2
  20.0 0.7 tile.4
  20.7 0.8 broadcast_in_dim_tile.8.b1
  21.5 2.3 %multiply_bitcast_fusion.1 = bf16[2,4,64,32]{0,3,1,2:T(8,128)(2,1)S(1)} fusion(bf16[64,4,32,256]{3,2,1,0:T(8,128)(2,1)} %vol.1, bf16[32,2]{1,0:T(8,128)(2,1)S(1)} %slice.113), kind=kLoop, calls=%fused_computation.1 | loop fusion | flops 16384 | bytes 65664 | tf_op jit(solution)/shard_map/transpose | solution.py:161
  23.7 2.4 %copy.79 = bf16[2,4,64,32]{2,1,0,3:T(4,128)(2,1)S(1)} copy(bf16[2,4,64,32]{0,3,1,2:T(8,128)(2,1)S(1)} %multiply_bitcast_fusion.1) | data formatting | bytes 65536 | tf_op jit(solution)/shard_map/transpose | solution.py:161
  26.1 0.1 reshape.105
  26.3 1.8 %multiply_bitcast_fusion = bf16[1,4,64,32]{0,3,1,2:T(8,128)(2,1)S(1)} fusion(bf16[64,4,32,256]{3,2,1,0:T(8,128)(2,1)} %vol.1, bf16[32]{0:T(256)(128)(2,1)S(1)} %slice_reduce_fusion), kind=kLoop, calls=%fused_computation | loop fusion | flops 8192 | bytes 32832 | tf_op jit(solution)/shard_map/transpose | solution.py:161
  28.1 2.4 %copy.82 = bf16[1,4,64,32]{2,1,3,0:T(4,128)(2,1)S(1)} copy(bf16[1,4,64,32]{0,3,1,2:T(8,128)(2,1)S(1)} %multiply_bitcast_fusion) | data formatting | bytes 32768 | tf_op jit(solution)/shard_map/transpose | solution.py:161
  30.5 0.1 reshape.106
  30.6 0.7 fusion.13
  31.3 0.1 copy.88
  31.4 0.1 add_convert_fusion
  31.5 4.5 %collective-permute-start.5 = (s32[5,1]{1,0:T(8,128)S(1)}, s32[5,1]{1,0:T(8,128)S(1)}, u32[]{:S(2)}, u32[]{:S(2)}) collective-permute-start(s32[5,1]{1,0:T(8,128)S(1)} %slice.109), channel_id=1, source_target_pairs={{0,4},{4,8},{8,12},{12,16},{16,20},{20,24},{24,28},{1,5},{5,9},{9,... | collective-permute-start | bytes 68 | tf_op jit(solution)/shard_map/ppermute | solution.py:178
  36.1 0.6 pad.13.row_mask
  36.8 0.1 slice_reduce_fusion.1
  37.0 0.1 concatenate.47
  37.1 0.5 slice.110
  37.6 0.5 pad_maximum_fusion.1
  38.1 0.2 copy.78
  38.3 0.1 slice_bitcast_fusion.2
  38.4 0.1 slice_bitcast_fusion.1
  38.5 0.1 copy.84
  38.6 0.1 copy.81
  38.7 0.1 copy.83
  38.8 0.1 copy.80
  39.0 4.2 %collective-permute-start.2 = (bf16[2,256,35]{1,0,2:T(2,128)(2,1)S(1)}, bf16[2,256,35]{1,0,2:T(2,128)(2,1)S(1)}, u32[]{:S(2)}, u32[]{:S(2)}) collective-permute-start(bf16[2,256,35]{1,0,2:T(2,128)(2,1)S(1)} %pad_maximum_fusion.4), channel_id=1, source_target_pairs={{0,4},{4,8},{8,12},{12,16},{16,20},{20,24},{24,28},{1,5},{5,9},{9,... | collective-permute-start | bytes 107528 | tf_op jit(solution)/shard_map/ppermute | solution.py:168
  43.3 2.1 %collective-permute-start.3 = (bf16[1,256,35]{1,2,0:T(8,128)(2,1)S(1)}, bf16[1,256,35]{1,2,0:T(8,128)(2,1)S(1)}, u32[]{:S(2)}, u32[]{:S(2)}) collective-permute-start(bf16[1,256,35]{1,2,0:T(8,128)(2,1)S(1)} %pad_maximum_fusion.5), channel_id=1, source_target_pairs={{4,0},{8,4},{12,8},{16,12},{20,16},{24,20},{28,24},{5,1},{9,5},{13... | collective-permute-start | bytes 53768 | tf_op jit(solution)/shard_map/ppermute | solution.py:169
  45.4 0.7 add_convert_fusion.1
  46.1 0.5 pad.14.col_mask
  46.7 1.7 %collective-permute-done.3 = bf16[1,256,35]{1,2,0:T(8,128)(2,1)S(1)} collective-permute-done((bf16[1,256,35]{1,2,0:T(8,128)(2,1)S(1)}, bf16[1,256,35]{1,2,0:T(8,128)(2,1)S(1)}, u32[]{:S(2)}, u32[]{:S(2)}) %collective-permute-start.3) | collective-permute-done | bytes 17952 | tf_op jit(solution)/shard_map/ppermute | solution.py:169
  48.4 0.1 pad_maximum_fusion.2
  48.6 0.2 copy.87
  48.9 0.2 pad_slice_fusion.2
  49.0 0.7 maximum_convert_fusion.sides
  49.8 0.8 pad_maximum_fusion.column
  50.6 52.7 %shard_map.95 = (bf16[64,4,16,128]{3,2,1,0:T(8,128)(2,1)}, bf16[32,64,128]{2,1,0:T(8,128)(2,1)}) custom-call(bf16[64,4,32,256]{3,2,1,0:T(8,128)(2,1)} %vol.1, bf16[32,256]{1,0:T(8,128)(2,1)} %copy-done.1, bf16[3,256,256]{2,1,0:T(8,128)(2,1)} %bitcast.38, f32[2,256,128]{2,1,0:T(8,128)} %maximum_convert_fusion.sides, ...), custom_call_target="tpu_custom_call" | custom-call | tf_op jit(solution)/shard_map/pallas_call | solution.py:196
  103.3 20.8 %all_to_all.5 = bf16[32,64,128]{2,1,0:T(8,128)(2,1)S(1)} all-to-all(bf16[32,64,128]{2,1,0:T(8,128)(2,1)} %get-tuple-element.5), channel_id=1, replica_groups=mesh['gx'=8,'gy'=4] {'gx','gy'}, dimensions={0} | all-to-all | bytes 1048576 | tf_op jit(solution)/shard_map/all_to_all | solution.py:220
  124.1 0.1 convert_reduce_fusion
  124.2 0.6 broadcast_multiply_fusion
  (29 shorter events, 0.6 us)
Async XLA Ops:
  1.3 30.0 %collective-permute-start.4 = (s32[1,8]{1,0:T(1,128)S(1)}, s32[1,8]{1,0:T(1,128)S(1)}, u32[]{:S(2)}, u32[]{:S(2)}) collective-permute-start(s32[1,8]{1,0:T(1,128)S(1)} %slice.108), channel_id=1, source_target_pairs={{0,1},{1,2},{2,3},{4,5},{5,6},{6,7},{8,9},{9,10},{10,11},{12,13},{... | collective-permute-start | bytes 104 | tf_op jit(solution)/shard_map/ppermute | solution.py:176
  8.0 29.6 %collective-permute-start.1 = (bf16[1,4,64,256]{3,0,1,2:T(2,128)(2,1)S(1)}, bf16[1,4,64,256]{3,0,1,2:T(2,128)(2,1)S(1)}, u32[]{:S(2)}, u32[]{:S(2)}) collective-permute-start(bf16[1,4,64,256]{3,0,1,2:T(2,128)(2,1)S(1)} %multiply_bitcast_fusion.2), channel_id=1, source_target_pairs={{1,0},{2,1},{3,2},{5,4},{6,5},{7,6},{9,8},{10,9},{11,10},{13,12},{... | collective-permute-start | bytes 393224 | tf_op jit(solution)/shard_map/ppermute | solution.py:157
  11.2 26.3 %collective-permute-start = (bf16[2,4,64,256]{3,0,1,2:T(2,128)(2,1)S(1)}, bf16[2,4,64,256]{3,0,1,2:T(2,128)(2,1)S(1)}, u32[]{:S(2)}, u32[]{:S(2)}) collective-permute-start(bf16[2,4,64,256]{3,0,1,2:T(2,128)(2,1)S(1)} %multiply_bitcast_fusion.3), channel_id=1, source_target_pairs={{0,1},{1,2},{2,3},{4,5},{5,6},{6,7},{8,9},{9,10},{10,11},{12,13},{... | collective-permute-start | bytes 786440 | tf_op jit(solution)/shard_map/ppermute | solution.py:156
  15.6 8.2 %copy-start.1 = (bf16[32,256]{1,0:T(8,128)(2,1)}, bf16[32,256]{1,0:T(8,128)(2,1)S(1)}, u32[]{:S(2)}) copy-start(bf16[32,256]{1,0:T(8,128)(2,1)S(1)} %convert_element_type.37.mask) | copy-start | bytes 49156
  28.1 3.4 %copy-start.2 = (s32[4,8]{1,0:T(4,128)S(1)}, s32[4,8]{1,0:T(4,128)}, u32[]{:S(2)}) copy-start(s32[4,8]{1,0:T(4,128)} %param.9) | copy-start | bytes 388
  31.5 5.3 %collective-permute-start.5 = (s32[5,1]{1,0:T(8,128)S(1)}, s32[5,1]{1,0:T(8,128)S(1)}, u32[]{:S(2)}, u32[]{:S(2)}) collective-permute-start(s32[5,1]{1,0:T(8,128)S(1)} %slice.109), channel_id=1, source_target_pairs={{0,4},{4,8},{8,12},{12,16},{16,20},{20,24},{24,28},{1,5},{5,9},{9,... | collective-permute-start | bytes 68 | tf_op jit(solution)/shard_map/ppermute | solution.py:178
  38.3 12.3 %copy-start = (bf16[3,4,64,256]{3,2,1,0:T(8,128)(2,1)}, bf16[3,4,64,256]{3,2,1,0:T(8,128)(2,1)S(1)}, u32[]{:S(2)}) copy-start(bf16[3,4,64,256]{3,2,1,0:T(8,128)(2,1)S(1)} %copy.78) | copy-start | bytes 1179652
  39.0 9.3 %collective-permute-start.2 = (bf16[2,256,35]{1,0,2:T(2,128)(2,1)S(1)}, bf16[2,256,35]{1,0,2:T(2,128)(2,1)S(1)}, u32[]{:S(2)}, u32[]{:S(2)}) collective-permute-start(bf16[2,256,35]{1,0,2:T(2,128)(2,1)S(1)} %pad_maximum_fusion.4), channel_id=1, source_target_pairs={{0,4},{4,8},{8,12},{12,16},{16,20},{20,24},{24,28},{1,5},{5,9},{9,... | collective-permute-start | bytes 107528 | tf_op jit(solution)/shard_map/ppermute | solution.py:168
  43.3 5.1 %collective-permute-start.3 = (bf16[1,256,35]{1,2,0:T(8,128)(2,1)S(1)}, bf16[1,256,35]{1,2,0:T(8,128)(2,1)S(1)}, u32[]{:S(2)}, u32[]{:S(2)}) collective-permute-start(bf16[1,256,35]{1,2,0:T(8,128)(2,1)S(1)} %pad_maximum_fusion.5), channel_id=1, source_target_pairs={{4,0},{8,4},{12,8},{16,12},{20,16},{24,20},{28,24},{5,1},{9,5},{13... | collective-permute-start | bytes 53768 | tf_op jit(solution)/shard_map/ppermute | solution.py:169

commit v3 on v2

v3 whole, which is shorter than its diff:
```python
import functools

import jax
import jax.numpy as jnp
from jax import lax
from jax.experimental import pallas as pl
from jax.experimental.pallas import tpu as pltpu
from jax.sharding import PartitionSpec as P

BY = 8
BX = 32
SEG_DEV = 128
PER = 2


def push(source, target, send, recv, axis, step):
    me, size = lax.axis_index(axis), lax.axis_size(axis)
    to = jnp.clip(me + step, 0, size - 1)
    has_to = (me + step >= 0) & (me + step < size)
    has_from = (me - step >= 0) & (me - step < size)
    copy = pltpu.make_async_remote_copy(
        src_ref=source, dst_ref=target, send_sem=send, recv_sem=recv,
        device_id={axis: to}, device_id_type=pl.DeviceIdType.MESH,
    )

    def start():
        @pl.when(has_to)
        def _():
            copy.start()

    def wait():
        @pl.when(has_to)
        def _():
            copy.wait_send()

        @pl.when(has_from)
        def _():
            copy.wait_recv()

    return start, wait


def greet():
    barrier = pltpu.get_barrier_semaphore()
    count = jnp.int32(0)
    for axis in ("gx", "gy"):
        me, size = lax.axis_index(axis), lax.axis_size(axis)
        for step in (-1, 1):
            there = (me + step >= 0) & (me + step < size)
            count = count + there.astype(jnp.int32)

            @pl.when(there)
            def _():
                pl.semaphore_signal(
                    barrier, inc=1, device_id={axis: jnp.clip(me + step, 0, size - 1)},
                    device_id_type=pl.DeviceIdType.MESH,
                )
    pl.semaphore_wait(barrier, count)


def block_kernel(
    vol, mask, wt1, wt2, bias1, bias2, own_mask, own_side, owners, segments,
    coarse, part,
    parted, src, hid, w1, w2, feats, flat, spread, hot, acc,
    halo, cols, cols_a, cols_b, got_a, got_b, sides, column, row_mask, top_mask, side_mask,
    left_mask, edge, send, recv,
):
    f32, bf16 = jnp.float32, jnp.bfloat16
    c, z, ny, nx = vol.shape
    half = nx // 2
    cz = c * z
    depth = 3 * cz

    def dot(a, b):
        return jnp.dot(a, b, preferred_element_type=f32)

    for ref in (halo, got_a, got_b, top_mask, left_mask, cols):
        ref[...] = jnp.zeros_like(ref)
    greet()

    at = lax.broadcasted_iota(jnp.int32, (nx, nx), 0)
    to = lax.broadcasted_iota(jnp.int32, (nx, nx), 1)
    sort = (at == jnp.where(to < half, 2 * to, 2 * to - nx + 1)).astype(f32).astype(bf16)
    lane = lax.broadcasted_iota(jnp.int32, (1, half), 1)

    def place(s, tap, first):
        return pl.ds(pl.multiple_of(s * depth + tap * cz + first, 64), c)

    def put_row(s, first, even, odd):
        here = pl.ds(first, c)
        there = lane == s
        last = lax.rem(s + 1, half)
        cols[0, here, :] = jnp.where(there, pltpu.roll(even, last, 1), cols[0, here, :])
        cols[1, here, :] = jnp.where(there, pltpu.roll(odd, last, 1), cols[1, here, :])
        cols[2, here, :] = jnp.where(there, pltpu.roll(even, s, 1), cols[2, here, :])
        even, odd = even.astype(bf16), odd.astype(bf16)
        src[place(s, 0, first), pl.ds(half, half)] = even
        src[place(s, 1, first), pl.ds(0, half)] = even
        src[place(s, 1, first), pl.ds(half, half)] = odd
        src[place(s, 2, first), pl.ds(0, half)] = odd

    def widen(s):
        for first in range(0, cz, c):
            even = src[place(s, 1, first), pl.ds(0, half)].astype(f32)
            odd = src[place(s, 1, first), pl.ds(half, half)].astype(f32)
            left = pltpu.roll(sides[0, pl.ds(first, c), :], lax.rem(half - s, half), 1)
            right = pltpu.roll(sides[1, pl.ds(first, c), :], half - 1 - s, 1)
            before = jnp.where(lane == 0, left, pltpu.roll(odd, 1, 1))
            after = jnp.where(lane == half - 1, right, pltpu.roll(even, half - 1, 1))
            src[place(s, 0, first), pl.ds(0, half)] = before.astype(bf16)
            src[place(s, 2, first), pl.ds(half, half)] = after.astype(bf16)

    for plane in range(z):
        block = (vol[:, plane] * mask[...][None]).reshape(c * ny, nx)
        both = dot(block, sort)
        parted[0] = both[:, :half]
        parted[1] = both[:, half:]

        @pl.loop(0, ny)
        def _(y):
            take = pl.ds(y, c, stride=ny)
            put_row(y + 2, plane * c, parted[0, take, :], parted[1, take, :])

    def line(s):
        return src.at[pl.ds(s * depth + cz, cz), :]

    rows = [
        push(line(ny), halo.at[0], send.at[0], recv.at[0], "gy", 1),
        push(line(ny + 1), halo.at[1], send.at[1], recv.at[1], "gy", 1),
        push(line(2), halo.at[2], send.at[2], recv.at[2], "gy", -1),
        push(own_mask.at[pl.ds(ny - 8, 8), :], top_mask, send.at[3], recv.at[3], "gy", 1),
    ]
    cols_a[...] = cols[...].astype(bf16)
    near = [
        push(cols_a.at[1], got_a.at[0], send.at[4], recv.at[4], "gx", 1),
        push(cols_a.at[2], got_a.at[1], send.at[5], recv.at[5], "gx", -1),
    ]
    for start, wait in near + rows:
        start()

    w1[...] = jnp.zeros_like(w1)
    w2[...] = jnp.zeros_like(w2)
    for tap in range(9):
        for zo in range(z):
            for zi in range(max(0, zo - 1), min(z, zo + 2)):
                w1[pl.ds(zo * c, c), pl.ds(tap * cz + zi * c, c)] = wt1[(zi - zo + 1) * 9 + tap]
            w2[pl.ds(zo * c, c), pl.ds(tap * cz + zo * c, c)] = wt2[tap]
    b1 = jnp.concatenate([bias1[...]] * z, 0)
    b2 = jnp.concatenate([bias2[...]] * z, 0)
    row_mask[pl.ds(1, ny), :] = own_mask[...]

    for start, wait in near:
        wait()
    sides[...] = got_a[...].astype(f32)

    @pl.loop(2, ny + 2)
    def _(s):
        widen(s)

    def hidden_row(t, places):
        got = dot(w1[...], src[pl.ds(pl.multiple_of(t * depth, depth), 3 * depth), :])
        got = jnp.maximum(got + b1, 0.0)
        keep = row_mask[pl.ds(t, 1), :]
        even = got[:, :half] * keep
        odd = got[:, half:] * keep
        parts = (pltpu.roll(odd, 1, 1).astype(bf16), even.astype(bf16), odd.astype(bf16))
        for p, dy, side in places:
            for tap in range(3):
                where = pl.multiple_of((p * 9 + dy * 3 + tap) * cz, cz)
                hid[pl.ds(where, cz), pl.ds(side * half, half)] = parts[tap]

    def four_rows(p):
        t = 4 * p + 1
        hidden_row(t, ((p, 1, 0),))
        hidden_row(t + 1, ((p, 2, 0), (p, 0, 1)))
        hidden_row(t + 2, ((p, 1, 1),))
        hidden_row(t + 3, ((p, 2, 1), (p + 1, 0, 0)))

    quads = ny // 4

    @pl.loop(1, quads // 2 + 1)
    def _(p):
        four_rows(p)

    for start, wait in rows:
        wait()
    for number, s in enumerate((0, 1, ny + 2)):
        for first in range(0, cz, c):
            both = halo[number, pl.ds(first, c), :].astype(f32)
            put_row(s, first, both[:, :half], both[:, half:])
    row_mask[pl.ds(0, 1), :] = top_mask[pl.ds(7, 1), :]
    cols_b[...] = cols[...].astype(bf16)
    side_mask[...] = jnp.where(
        lane == 0, pltpu.roll(jnp.broadcast_to(top_mask[pl.ds(7, 1), :], (8, half)), 1, 1),
        own_side[...],
    )
    far = [
        push(cols_b.at[pl.ds(0, 2)], got_b.at[pl.ds(0, 2)], send.at[6], recv.at[6], "gx", 1),
        push(cols_b.at[2], got_b.at[2], send.at[7], recv.at[7], "gx", -1),
        push(side_mask, left_mask, send.at[8], recv.at[8], "gx", 1),
    ]
    for start, wait in far:
        start()

    @pl.loop(quads // 2 + 1, quads - 1)
    def _(p):
        four_rows(p)

    for start, wait in far:
        wait()
    sides[...] = got_b[pl.ds(1, 2)].astype(f32)
    for s in (0, 1, ny + 2):
        widen(s)

    for dx in range(3):
        wide = cols[2] if dx == 2 else got_b[dx].astype(f32)
        for dy in range(3):
            moved = wide if dy == 0 else pltpu.roll(wide, half - dy, 1)
            column[pl.ds((dy * 3 + dx) * cz, cz), :] = moved.astype(bf16)
    got = dot(w1[...], column[...])
    edge[...] = jnp.maximum(got + b1, 0.0) * left_mask[pl.ds(0, 1), :]
    hidden_row(0, ((0, 0, 0),))

    @pl.loop(0, 2)
    def _(i):
        four_rows(i * (quads - 1))

    @pl.loop(0, quads)
    def _(p):
        for dy in range(3):
            for side in range(2):
                t = 4 * p + 2 * side + dy
                spot = pl.ds(pl.multiple_of((p * 9 + dy * 3) * cz, cz), cz)
                first = pltpu.roll(edge[...], lax.rem(half - t, half), 1)
                old = hid[spot, pl.ds(side * half, half)].astype(f32)
                hid[spot, pl.ds(side * half, half)] = jnp.where(lane == 0, first, old).astype(bf16)
        got = dot(w2[...], hid[pl.ds(pl.multiple_of(p * 9 * cz, cz), 9 * cz), :])
        got = jnp.maximum(got + b2, 0.0).astype(bf16)
        feats[:, pl.ds(pl.multiple_of(p * nx, nx), nx)] = got
        wide = got.astype(f32)
        flat[pl.ds(2 * p, cz, stride=ny // 2), :] = wide[:, :half]
        flat[pl.ds(2 * p + 1, cz, stride=ny // 2), :] = wide[:, half:]

    for plane in range(z):
        piece = flat[pl.ds(plane * c * ny // 2, c * ny // 2), :]
        coarse[:, plane] = piece.reshape(c, ny // 2, half).astype(bf16)

    voxels = feats.shape[1]
    groups = part.shape[0] // PER
    chunk = spread.shape[0] // c

    @pl.loop(0, groups // chunk)
    def _(g):
        for plane in range(z):
            which = lax.rem(owners[pl.ds(plane, 1), :], PER) * SEG_DEV + segments[pl.ds(plane, 1), :]
            ids = lax.broadcasted_iota(jnp.int32, (PER * SEG_DEV, 1), 0)
            hot[...] = (ids == which).astype(f32).astype(bf16)
            owner = owners[pl.ds(plane, 1), :] // PER
            for a in range(chunk):
                on = (owner == g * chunk + a).astype(f32).astype(bf16)
                spread[pl.ds(a * c, c), :] = feats[pl.ds(plane * c, c), :] * on
            got = lax.dot_general(
                spread[...], hot[...], (((1,), (1,)), ((), ())), preferred_element_type=f32
            )
            if plane == 0:
                acc[...] = got
            else:
                acc[...] += got
        for a in range(chunk):
            for n in range(PER):
                part[(g * chunk + a) * PER + n] = acc[
                    pl.ds(a * c, c), pl.ds(n * SEG_DEV, SEG_DEV)
                ].astype(bf16)


def reduce_kernel(part, out, mine, got_x, got_y, send_x, recv_x, send_y, recv_y):
    f32, bf16 = jnp.float32, jnp.bfloat16
    x, y = lax.axis_index("gx"), lax.axis_index("gy")
    size_x, size_y = lax.axis_size("gx"), lax.axis_size("gy")
    barrier = pltpu.get_barrier_semaphore()
    for i in range(1, size_x):
        pl.semaphore_signal(
            barrier, inc=1, device_id={"gx": lax.rem(x + i, size_x)},
            device_id_type=pl.DeviceIdType.MESH,
        )
    for i in range(1, size_y):
        pl.semaphore_signal(
            barrier, inc=1, device_id={"gy": lax.rem(y + i, size_y)},
            device_id_type=pl.DeviceIdType.MESH,
        )
    pl.semaphore_wait(barrier, size_x + size_y - 2)

    def spread(axis, me, size, source, target, send, recv):
        copies = []
        for i in range(1, size):
            to = lax.rem(me + i, size)
            copy = pltpu.make_async_remote_copy(
                src_ref=source.at[to], dst_ref=target.at[i], send_sem=send.at[i],
                recv_sem=recv.at[i], device_id={axis: to},
                device_id_type=pl.DeviceIdType.MESH,
            )
            copy.start()
            copies.append(copy)
        for copy in copies:
            copy.wait()

    spread("gx", x, size_x, part, got_x, send_x, recv_x)
    total = part[x].astype(f32)
    for i in range(1, size_x):
        total = total + got_x[i].astype(f32)
    mine[...] = total.astype(bf16)
    spread("gy", y, size_y, mine, got_y, send_y, recv_y)
    sums = mine[y].astype(f32)
    for i in range(1, size_y):
        sums = sums + got_y[i].astype(f32)
    out[...] = sums * lax.rsqrt(jnp.mean(sums * sums, axis=0, keepdims=True) + 1e-05)


def per_device(volume, brick_mask, w1, b1, w2, b2, voxel_owner, voxel_segment):
    c, z, ny, nx = volume.shape
    bf16, f32 = jnp.bfloat16, jnp.float32
    half, cz = nx // 2, c * z
    size_x, size_y = lax.axis_size("gx"), lax.axis_size("gy")
    devices = size_x * size_y
    tall = jnp.repeat(brick_mask, BY, 0)
    mask = jnp.repeat(tall, BX, 1).astype(bf16)
    own_mask = jnp.repeat(tall, BX // 2, 1).astype(f32)
    own_side = jnp.pad(tall[:, -1], (1, half - ny - 1)).astype(f32)
    own_side = jnp.broadcast_to(own_side[None], (8, half))
    wt1 = w1.transpose(2, 3, 4, 0, 1).reshape(27, c, c)
    wt2 = w2[:, :, 0].transpose(2, 3, 0, 1).reshape(9, c, c)
    owner = voxel_owner.reshape(z, -1)
    segment = voxel_segment.reshape(z, -1)
    voxels = owner.shape[1]
    groups = devices // PER
    chunk = min(groups, 16)

    coarse, part = pl.pallas_call(
        block_kernel,
        out_shape=(
            jax.ShapeDtypeStruct((c, z, ny // 2, half), bf16),
            jax.ShapeDtypeStruct((devices, c, SEG_DEV), bf16),
        ),
        in_specs=[pl.BlockSpec(memory_space=pltpu.VMEM)] * 10,
        out_specs=[pl.BlockSpec(memory_space=pltpu.VMEM)] * 2,
        scratch_shapes=[
            pltpu.VMEM((2, c * ny, half), f32),
            pltpu.VMEM(((ny + 3) * 3 * cz, nx), bf16),
            pltpu.VMEM(((ny // 4 * 9 + 3) * cz, nx), bf16),
            pltpu.VMEM((cz, 9 * cz), bf16),
            pltpu.VMEM((cz, 9 * cz), bf16),
            pltpu.VMEM((cz, voxels), bf16),
            pltpu.VMEM((cz * ny // 2, half), f32),
            pltpu.VMEM((chunk * c, voxels), bf16),
            pltpu.VMEM((PER * SEG_DEV, voxels), bf16),
            pltpu.VMEM((chunk * c, PER * SEG_DEV), f32),
            pltpu.VMEM((3, cz, nx), bf16),
            pltpu.VMEM((3, cz, half), f32),
            pltpu.VMEM((3, cz, half), bf16),
            pltpu.VMEM((3, cz, half), bf16),
            pltpu.VMEM((2, cz, half), bf16),
            pltpu.VMEM((3, cz, half), bf16),
            pltpu.VMEM((2, cz, half), f32),
            pltpu.VMEM((9 * cz, half), bf16),
            pltpu.VMEM((ny + 8, half), f32),
            pltpu.VMEM((8, half), f32),
            pltpu.VMEM((8, half), f32),
            pltpu.VMEM((8, half), f32),
            pltpu.VMEM((cz, half), f32),
            pltpu.SemaphoreType.DMA((9,)),
            pltpu.SemaphoreType.DMA((9,)),
        ],
        compiler_params=pltpu.CompilerParams(
            collective_id=0, has_side_effects=True, vmem_limit_bytes=58 * 1024 * 1024
        ),
    )(volume, mask, wt1, wt2, b1[:, None], b2[:, None], own_mask, own_side, owner, segment)
    supervox = pl.pallas_call(
        reduce_kernel,
        out_shape=jax.ShapeDtypeStruct((c, SEG_DEV), f32),
        in_specs=[pl.BlockSpec(memory_space=pltpu.VMEM)],
        out_specs=pl.BlockSpec(memory_space=pltpu.VMEM),
        scratch_shapes=[
            pltpu.VMEM((size_y, c, SEG_DEV), bf16),
            pltpu.VMEM((size_x, size_y, c, SEG_DEV), bf16),
            pltpu.VMEM((size_y, c, SEG_DEV), bf16),
            pltpu.SemaphoreType.DMA((size_x,)),
            pltpu.SemaphoreType.DMA((size_x,)),
            pltpu.SemaphoreType.DMA((size_y,)),
            pltpu.SemaphoreType.DMA((size_y,)),
        ],
        compiler_params=pltpu.CompilerParams(
            collective_id=1, has_side_effects=True, vmem_limit_bytes=32 * 1024 * 1024
        ),
    )(part.reshape(size_x, size_y, c, SEG_DEV))
    return (coarse, supervox)


def solution(mesh):
    placed = (
        P(None, None, "gy", "gx"),
        P("gy", "gx"),
        P(),
        P(),
        P(),
        P(),
        P(("gx", "gy"), None),
        P(("gx", "gy")),
    )
    return jax.shard_map(
        per_device,
        mesh=mesh,
        in_specs=placed,
        out_specs=(P(None, None, "gy", "gx"), P(None, ("gx", "gy"))),
        check_vma=False,
    )
```

time: 126 us -> 97.3 us (0.77)
  Pallas kernels: 52.7 us -> 82 us
  blocking collectives: 20.8 us -> 0 us
  starting transfers between devices: 20.1 us -> 0 us
  other arithmetic: 13.2 us -> 1.56 us
  local copies, waits for them, and re-layouts: 15.4 us -> 12.3 us
  waiting for transfers between devices: 1.72 us -> 0 us
    all_to_all x1 -> x0, blocking collectives: 20.8 us -> none  [per_device(): lax.all_to_all(part, ('gx', 'gy'), split_axis=0, concat_axis=0, tiled=True)]
    ppermute x6 -> x0, starting transfers between devices: 20.1 us -> none  [the longest x1 4.51 us: per_device(): marks_x = lax.ppermute(bricks[:, -1:], 'gx', right_way)]
    pallas_call x0 -> x1, Pallas kernels: none -> 14.7 us  [per_device(): pl.pallas_call(reduce_kernel, out_shape=jax.ShapeDtypeStruct((c, SEG_DEV)...]
    pallas_call x1, Pallas kernels: 52.7 us -> 67.2 us  [per_device(): pl.pallas_call(block_kernel, out_shape=(jax.ShapeDtypeStruct((c, z, ny //...]
    transpose x4 -> x0, other arithmetic: 7.12 us -> none  [the longest x2 4.06 us: columns(): mine = planes(0, ny, x0, x1).transpose(3, 1, 0, 2).reshape(x1 - x0, cz, ny)]
    transpose x8 -> x0, local copies, waits for them, and re-layouts: 5.35 us -> none  [the longest x2 4.81 us: columns(): mine = planes(0, ny, x0, x1).transpose(3, 1, 0, 2).reshape(x1 - x0, cz, ny)]
    unnamed x8 -> x6, local copies, waits for them, and re-layouts: 1.29 us -> 5.3 us
    broadcast_in_dim x6, local copies, waits for them, and re-layouts: 0.4 us -> 3.49 us  [the longest x1 1.36 us: per_device(): b1[:, None]]
  transfers between devices with their start and end apart: 6 -> 0, of which waited for: 1 -> 0; matrix products, arithmetic and copies ran while one was open for 19% -> 0% of each run, Pallas kernels for 0% -> 0%
where the time goes in v3:
time: 97.3 us; the launch traced here: 96.5 us
  Pallas kernels  82 us (84%)
  local copies, waits for them, and re-layouts  12.3 us (13%)
  other arithmetic  1.56 us (2%)
    pallas_call x1, Pallas kernels, per_device(): pl.pallas_call(block_kernel, out_shape=(jax.ShapeDtypeStruct((c, z, ny //...  67.2 us
    pallas_call x1, Pallas kernels, per_device(): pl.pallas_call(reduce_kernel, out_shape=jax.ShapeDtypeStruct((c, SEG_DEV)...  14.7 us
    unnamed x6, local copies, waits for them, and re-layouts  5.3 us

profile of v3, /device:TPU:1, one launch (start us, length us, event | category | flops | bytes accessed | tf_op | source)
XLA Modules:
  0.0 96.5 jit_solution(16637802913936827522)
XLA Ops:
  0.6 0.8 copy.15
  1.4 0.1 broadcast_in_dim.21
  1.5 0.1 reshape.27
  1.6 0.1 pad_convert_fusion
  1.6 0.6 broadcast_in_dim.26.own_side
  2.2 0.1 copy.16
  2.3 0.5 broadcast.8
  2.8 1.5 %reduce.3 = s32[8192]{0:T(1024)S(1)} reduce(s32[8192,1]{0,1:T(1,128)} %param.14, s32[]{:T(128)} %broadcast.8), dimensions={1}, to_apply=%param.14.reduce_sub_computation.3 | reduce | bytes 65540 | tf_op args[6]
  4.3 0.6 reshape.30.owners
  4.9 1.4 %copy.17.bias1 = f32[64,1]{1,0:T(8,128)} copy(f32[64,1]{0,1:T(1,128)} %bitcast.21) | data formatting | bytes 512 | tf_op jit(solution)/shard_map/broadcast_in_dim | solution.py:376
  6.3 1.4 %copy.18.bias2 = f32[64,1]{1,0:T(8,128)} copy(f32[64,1]{0,1:T(1,128)} %bitcast.22) | data formatting | bytes 512 | tf_op jit(solution)/shard_map/broadcast_in_dim | solution.py:376
  7.7 1.4 %reshape.31.segments = s32[4,2048]{1,0:T(4,128)} reshape(s32[8192]{0:T(1024)} %param.15) | data formatting | bytes 65536 | tf_op jit(solution)/shard_map/reshape | solution.py:333
  9.0 0.1 broadcast_in_dim.22
  9.1 0.7 convert_element_type.14.mask
  9.8 0.7 copy.19.own_mask
  10.5 67.2 %shard_map.95 = (bf16[64,4,16,128]{3,2,1,0:T(8,128)(2,1)}, bf16[32,64,128]{2,1,0:T(8,128)(2,1)}) custom-call(bf16[64,4,32,256]{3,2,1,0:T(8,128)(2,1)} %vol.1, bf16[32,256]{1,0:T(8,128)(2,1)} %convert_element_type.14.mask, bf16[27,64,64]{2,1,0:T(8,128)(2,1)} %bitcast.18, bf16[9,64,64]{2,1,0:T(8,128)(2,1)} %bitcast.20, f32[64,1]{1,0:T(8,128)} %copy.17.bias1, ...), custom_call_target="tpu_custom_call" | custom-call | tf_op jit(solution)/shard_map/pallas_call | solution.py:338
  77.8 0.0 copy-start
  77.8 1.0 %copy-done = bf16[32,64,128]{2,1,0:T(8,128)(2,1)S(1)} copy-done((bf16[32,64,128]{2,1,0:T(8,128)(2,1)S(1)}, bf16[32,64,128]{2,1,0:T(8,128)(2,1)}, u32[]{:S(2)}) %copy-start) | copy-done | bytes 524312
  78.8 14.7 %shard_map.96 = f32[64,128]{1,0:T(8,128)S(1)} custom-call(bf16[8,4,64,128]{3,2,1,0:T(8,128)(2,1)S(1)} %bitcast.17), custom_call_target="tpu_custom_call" | custom-call | tf_op jit(solution)/shard_map/pallas_call | solution.py:377
  93.5 2.4 %copy.22 = bf16[64,4,16,128]{3,2,1,0:T(8,128)(2,1)} copy(bf16[64,4,16,128]{3,2,1,0:T(8,128)(2,1)} %get-tuple-element.10) | data formatting | bytes 2097152
  95.9 0.6 copy.23
  (3 shorter events, 0.0 us)
Async XLA Ops:
  77.8 1.0 %copy-start = (bf16[32,64,128]{2,1,0:T(8,128)(2,1)S(1)}, bf16[32,64,128]{2,1,0:T(8,128)(2,1)}, u32[]{:S(2)}) copy-start(bf16[32,64,128]{2,1,0:T(8,128)(2,1)} %get-tuple-element.5) | copy-start | bytes 1572868

commit v4 on v3

--- a/solution.py
+++ b/solution.py
@@ -100,15 +100,16 @@
         src[place(s, 2, first), pl.ds(0, half)] = odd
 
     def widen(s):
-        for first in range(0, cz, c):
-            even = src[place(s, 1, first), pl.ds(0, half)].astype(f32)
-            odd = src[place(s, 1, first), pl.ds(half, half)].astype(f32)
-            left = pltpu.roll(sides[0, pl.ds(first, c), :], lax.rem(half - s, half), 1)
-            right = pltpu.roll(sides[1, pl.ds(first, c), :], half - 1 - s, 1)
-            before = jnp.where(lane == 0, left, pltpu.roll(odd, 1, 1))
-            after = jnp.where(lane == half - 1, right, pltpu.roll(even, half - 1, 1))
-            src[place(s, 0, first), pl.ds(0, half)] = before.astype(bf16)
-            src[place(s, 2, first), pl.ds(half, half)] = after.astype(bf16)
+        base = s * depth
+        middle = pl.ds(pl.multiple_of(base + cz, cz), cz)
+        even = src[middle, pl.ds(0, half)].astype(f32)
+        odd = src[middle, pl.ds(half, half)].astype(f32)
+        left = pltpu.roll(sides[0], lax.rem(half - s, half), 1)
+        right = pltpu.roll(sides[1], half - 1 - s, 1)
+        before = jnp.where(lane == 0, left, pltpu.roll(odd, 1, 1))
+        after = jnp.where(lane == half - 1, right, pltpu.roll(even, half - 1, 1))
+        src[pl.ds(pl.multiple_of(base, cz), cz), pl.ds(0, half)] = before.astype(bf16)
+        src[pl.ds(pl.multiple_of(base + 2 * cz, cz), cz), pl.ds(half, half)] = after.astype(bf16)
 
     for plane in range(z):
         block = (vol[:, plane] * mask[...][None]).reshape(c * ny, nx)
@@ -116,7 +117,7 @@
         parted[0] = both[:, :half]
         parted[1] = both[:, half:]
 
-        @pl.loop(0, ny)
+        @pl.loop(0, ny, unroll=4)
         def _(y):
             take = pl.ds(y, c, stride=ny)
             put_row(y + 2, plane * c, parted[0, take, :], parted[1, take, :])
@@ -145,8 +146,12 @@
             for zi in range(max(0, zo - 1), min(z, zo + 2)):
                 w1[pl.ds(zo * c, c), pl.ds(tap * cz + zi * c, c)] = wt1[(zi - zo + 1) * 9 + tap]
             w2[pl.ds(zo * c, c), pl.ds(tap * cz + zo * c, c)] = wt2[tap]
-    b1 = jnp.concatenate([bias1[...]] * z, 0)
-    b2 = jnp.concatenate([bias2[...]] * z, 0)
+    row = lax.broadcasted_iota(jnp.int32, (c, c), 0)
+    diagonal = row == lax.broadcasted_iota(jnp.int32, (c, c), 1)
+    b1, b2 = [
+        jnp.concatenate([jnp.sum(jnp.where(diagonal, bias[...], 0.0), 1, keepdims=True)] * z, 0)
+        for bias in (bias1, bias2)
+    ]
     row_mask[pl.ds(1, ny), :] = own_mask[...]
 
     for start, wait in near:
@@ -228,12 +233,15 @@
     @pl.loop(0, quads)
     def _(p):
         for dy in range(3):
+            spot = pl.ds(pl.multiple_of((p * 9 + dy * 3) * cz, cz), cz)
+            pair = []
             for side in range(2):
                 t = 4 * p + 2 * side + dy
-                spot = pl.ds(pl.multiple_of((p * 9 + dy * 3) * cz, cz), cz)
                 first = pltpu.roll(edge[...], lax.rem(half - t, half), 1)
                 old = hid[spot, pl.ds(side * half, half)].astype(f32)
-                hid[spot, pl.ds(side * half, half)] = jnp.where(lane == 0, first, old).astype(bf16)
+                pair.append(jnp.where(lane == 0, first, old).astype(bf16))
+            for side in range(2):
+                hid[spot, pl.ds(side * half, half)] = pair[side]
         got = dot(w2[...], hid[pl.ds(pl.multiple_of(p * 9 * cz, cz), 9 * cz), :])
         got = jnp.maximum(got + b2, 0.0).astype(bf16)
         feats[:, pl.ds(pl.multiple_of(p * nx, nx), nx)] = got
@@ -373,7 +381,7 @@
         compiler_params=pltpu.CompilerParams(
             collective_id=0, has_side_effects=True, vmem_limit_bytes=58 * 1024 * 1024
         ),
-    )(volume, mask, wt1, wt2, b1[:, None], b2[:, None], own_mask, own_side, owner, segment)
+    )(volume, mask, wt1, wt2, b1[None], b2[None], own_mask, own_side, owner, segment)
     supervox = pl.pallas_call(
         reduce_kernel,
         out_shape=jax.ShapeDtypeStruct((c, SEG_DEV), f32),

time: 97.3 us -> 80.1 us (0.82)
  Pallas kernels: 82 us -> 67.5 us
  local copies, waits for them, and re-layouts: 12.3 us -> 9.64 us
    pallas_call x1, Pallas kernels: 67.2 us -> 52.8 us  [per_device(): pl.pallas_call(block_kernel, out_shape=(jax.ShapeDtypeStruct((c, z, ny //...]
    broadcast_in_dim x2 -> x0, local copies, waits for them, and re-layouts: 2.71 us -> none  [the longest x1 1.36 us: per_device(): b1[:, None]]
where the time goes in v4:
time: 80.1 us; the launch traced here: 79.4 us
  Pallas kernels  67.5 us (84%)
  local copies, waits for them, and re-layouts  9.64 us (12%)
  other arithmetic  1.56 us (2%)
    pallas_call x1, Pallas kernels, per_device(): pl.pallas_call(block_kernel, out_shape=(jax.ShapeDtypeStruct((c, z, ny //...  52.8 us
    pallas_call x1, Pallas kernels, per_device(): pl.pallas_call(reduce_kernel, out_shape=jax.ShapeDtypeStruct((c, SEG_DEV)...  14.7 us
    unnamed x6, local copies, waits for them, and re-layouts  5.3 us

profile of v4, /device:TPU:1, one launch (start us, length us, event | category | flops | bytes accessed | tf_op | source)
XLA Modules:
  0.0 79.4 jit_solution(15265827209852287016)
XLA Ops:
  0.6 0.8 copy.13
  1.4 0.1 broadcast_in_dim.21
  1.5 0.1 reshape.27
  1.6 0.1 pad_convert_fusion
  1.6 0.6 broadcast_in_dim.26.own_side
  2.2 0.1 copy.14
  2.3 0.5 broadcast.8
  2.8 1.5 %reduce.3 = s32[8192]{0:T(1024)S(1)} reduce(s32[8192,1]{0,1:T(1,128)} %param.14, s32[]{:T(128)} %broadcast.8), dimensions={1}, to_apply=%param.14.reduce_sub_computation.3 | reduce | bytes 65540 | tf_op args[6]
  4.3 0.6 reshape.30.owners
  4.9 1.4 %reshape.31.segments = s32[4,2048]{1,0:T(4,128)} reshape(s32[8192]{0:T(1024)} %param.15) | data formatting | bytes 65536 | tf_op jit(solution)/shard_map/reshape | solution.py:341
  6.3 0.1 broadcast_in_dim.22
  6.4 0.7 convert_element_type.14.mask
  7.2 0.7 copy.15.own_mask
  7.8 52.8 %shard_map.95 = (bf16[64,4,16,128]{3,2,1,0:T(8,128)(2,1)}, bf16[32,64,128]{2,1,0:T(8,128)(2,1)}) custom-call(bf16[64,4,32,256]{3,2,1,0:T(8,128)(2,1)} %vol.1, bf16[32,256]{1,0:T(8,128)(2,1)} %convert_element_type.14.mask, bf16[27,64,64]{2,1,0:T(8,128)(2,1)} %bitcast.18, bf16[9,64,64]{2,1,0:T(8,128)(2,1)} %bitcast.20, f32[1,64]{1,0:T(1,128)} %bitcast.21, ...), custom_call_target="tpu_custom_call" | custom-call | tf_op jit(solution)/shard_map/pallas_call | solution.py:346
  60.6 0.0 copy-start
  60.7 1.0 %copy-done = bf16[32,64,128]{2,1,0:T(8,128)(2,1)S(1)} copy-done((bf16[32,64,128]{2,1,0:T(8,128)(2,1)S(1)}, bf16[32,64,128]{2,1,0:T(8,128)(2,1)}, u32[]{:S(2)}) %copy-start) | copy-done | bytes 524312
  61.7 14.7 %shard_map.96 = f32[64,128]{1,0:T(8,128)S(1)} custom-call(bf16[8,4,64,128]{3,2,1,0:T(8,128)(2,1)S(1)} %bitcast.17), custom_call_target="tpu_custom_call" | custom-call | tf_op jit(solution)/shard_map/pallas_call | solution.py:385
  76.4 2.4 %copy.18 = bf16[64,4,16,128]{3,2,1,0:T(8,128)(2,1)} copy(bf16[64,4,16,128]{3,2,1,0:T(8,128)(2,1)} %get-tuple-element.10) | data formatting | bytes 2097152
  78.8 0.6 copy.19
  (3 shorter events, 0.0 us)
Async XLA Ops:
  60.6 1.0 %copy-start = (bf16[32,64,128]{2,1,0:T(8,128)(2,1)S(1)}, bf16[32,64,128]{2,1,0:T(8,128)(2,1)}, u32[]{:S(2)}) copy-start(bf16[32,64,128]{2,1,0:T(8,128)(2,1)} %get-tuple-element.5) | copy-start | bytes 1572868
